TPU v7x, 128 devices: a whole 4x4x4 slice. The times are simulated.
128 devices in a mesh: dp: 2 (over core), expert: 64 (over z, y, x).
Axes of the slice: x: 4, y: 4, z: 4, core: 2. Of those that a mesh axis runs over, the one named last changes fastest.
Arguments:
- block_entry_states: bfloat16 [64, 256, 2048], P('expert', 'dp'), may hold values from -6 to 6
- block_result_cotangent: bfloat16 [64, 256, 2048], P('expert', 'dp'), may hold values from -6 to 6
- token_assignments: int32 [64, 256, 8], P('expert', 'dp'), may hold values from 0 to 63, all different within a row
- packed_segment_sizes: int32 [64, 4], P('expert'), may hold values from 1 to 192, 256 in all within a row
- admitted_route_quota: int32 [64], replicated, may hold values from 6 to 12, as said below
- mixing_scale_factor: float32 [2048], replicated, may hold values from 0.25 to 1.75
- asker_projection: bfloat16 [2048, 2048], P('expert', 'dp'), may hold values from -0.125 to 0.125
- lookup_projection: bfloat16 [2048, 2048], P('expert', 'dp'), may hold values from -0.125 to 0.125
- content_projection: bfloat16 [2048, 2048], P('expert', 'dp'), may hold values from -0.125 to 0.125
- mixing_projection_back: bfloat16 [2048, 2048], P(('dp', 'expert')), may hold values from -0.75 to 0.75
- asker_scale_factor: float32 [2048], replicated, may hold values from 0.3 to 2.8
- lookup_scale_factor: float32 [2048], replicated, may hold values from 0.3 to 2.8
- specialist_scale_factor: float32 [2048], replicated, may hold values from 0.25 to 1.75
- dispatcher_projection: bfloat16 [2048, 64], replicated, may hold values from -0.15625 to 0.15625
- specialist_switch_tensor: bfloat16 [64, 2048, 1024], P('expert'), may hold values from -0.125 to 0.125
- specialist_widen_tensor: bfloat16 [64, 2048, 1024], P('expert'), may hold values from -0.125 to 0.125
- specialist_shrink_tensor: bfloat16 [64, 1024, 2048], P('expert'), may hold values from -6 to 6
Outputs:
- block_output: float32 [64, 256, 2048], P('expert', 'dp')
- input_grad: float32 [64, 256, 2048], P('expert', 'dp')
- attn_gain_grad: float32 [2048], replicated
- query_weight_grad: float32 [2048, 2048], P('expert', 'dp')
- key_weight_grad: float32 [2048, 2048], P('expert', 'dp')
- value_weight_grad: float32 [2048, 2048], P('expert', 'dp')
- output_weight_grad: float32 [2048, 2048], P(('dp', 'expert'))
- query_gain_grad: float32 [2048], replicated
- key_gain_grad: float32 [2048], replicated
- moe_gain_grad: float32 [2048], replicated
- router_weight_grad: float32 [2048, 64], replicated
- gate_weight_grad: float32 [64, 2048, 1024], P('expert', None, 'dp')
- up_weight_grad: float32 [64, 2048, 1024], P('expert', None, 'dp')
- down_weight_grad: float32 [64, 1024, 2048], P('expert', 'dp')
- expert_counts: int32 [64, 128], P('expert', 'dp')
Inputs may be any that keep to these rules, and one draw needn't show every extreme that they name: `token_assignments`: each token names 8 different experts, and every expert is named by some token. `packed_segment_sizes`: the 4 lengths of a row sum to 256, and the longest is 192. `admitted_route_quota`: some expert accepts 12.
All inputs are finite; a program needn't handle non-finite values.
Results may differ from a plain program's by a relative error of at most 0.023.
Values may be sent and summed in bfloat16 or wider, within the bound.
No kernel may reach another device: no remote copies, remote signals or barrier semaphores. Data moves between devices by JAX's collectives and lax.ppermute only.
A program may use at most 256 MiB of HBM per device.

v0:
```python
import jax
import jax.numpy as jnp
from jax import lax
from jax.sharding import PartitionSpec as P

HEADS = 16


EPS = 1e-05
THETA = 10000.0
NEG = -1e30


def sent_together(arrays, axis, dim, along):
    widths = [a.shape[along] for a in arrays]
    both = jnp.concatenate(arrays, axis=along)
    whole = lax.all_gather(both, axis, axis=dim, tiled=True)
    return tuple(jnp.split(whole, [sum(widths[:k]) for k in range(1, len(widths))], axis=along))


def grouped_exchange(shard, axis, split_dim, concat_dim, work, item_dim, out_dim):
    items = jax.tree.leaves(shard)[0].shape[item_dim]
    count = 2 if items % 2 == 0 else 1
    done = []
    for k in range(count):
        group = jax.tree.map(
            lambda a: lax.slice_in_dim(
                a, k * (items // count), (k + 1) * (items // count), axis=item_dim
            ),
            shard,
        )
        done.append(
            work(
                lax.all_to_all(
                    group, axis, split_axis=split_dim, concat_axis=concat_dim, tiled=True
                )
            )
        )
    return jax.tree.map(lambda *parts: jnp.concatenate(parts, axis=out_dim), *done)


def sent_together_2(arrays, axis, dim, along):
    widths = [a.shape[along] for a in arrays]
    both = jnp.concatenate(arrays, axis=along)
    whole = lax.psum_scatter(both, axis, scatter_dimension=dim, tiled=True)
    return tuple(jnp.split(whole, [sum(widths[:k]) for k in range(1, len(widths))], axis=along))


def in_one(arrays, axis):
    ravelled, at, done = (jnp.concatenate([a.reshape(-1) for a in arrays]), 0, [])
    so_far = lax.psum(ravelled, axis)
    for a in arrays:
        done.append(so_far[at : at + a.size].reshape(a.shape))
        at += a.size
    return tuple(done)


def rms_factor(values):
    return lax.rsqrt(jnp.mean(values * values, axis=-1, keepdims=True) + EPS)


def norm_back(grad_normed, source, factor, gain):
    scaled = grad_normed * gain
    grad_source = factor * (
        scaled - source * factor * factor * jnp.mean(scaled * source, axis=-1, keepdims=True)
    )
    grad_gain = jnp.sum(grad_normed * source * factor, axis=0)
    return (grad_source, grad_gain)


def doc_places(lengths, places):
    ends = jnp.cumsum(lengths, dtype=jnp.int32)
    done = ends[None, :] <= places[:, None]
    doc_ids = jnp.sum(done.astype(jnp.int32), axis=1, dtype=jnp.int32)
    starts = jnp.sum(jnp.where(done, lengths[None, :], 0), axis=1, dtype=jnp.int32)
    return (doc_ids, places - starts)


def rope_tables(offsets, head_width):
    half_width = head_width // 2
    inverse = THETA ** (-jnp.arange(half_width, dtype=jnp.float32) * 2.0 / head_width)
    angles = offsets.astype(jnp.float32)[..., None] * inverse
    return (jnp.cos(angles)[..., None, :], jnp.sin(angles)[..., None, :])


def rotate(values, cos_table, sin_table):
    half_width = values.shape[-1] // 2
    first, second = (values[..., :half_width], values[..., half_width:])
    return jnp.concatenate(
        [first * cos_table - second * sin_table, second * cos_table + first * sin_table], axis=-1
    )


def unrotate(grads, cos_table, sin_table):
    half_width = grads.shape[-1] // 2
    first, second = (grads[..., :half_width], grads[..., half_width:])
    return jnp.concatenate(
        [first * cos_table + second * sin_table, second * cos_table - first * sin_table], axis=-1
    )


def softmax_rows(values):
    row_max = jnp.max(values, axis=-1, keepdims=True)
    exponent = jnp.exp(values - row_max)
    totals = jnp.sum(exponent, axis=-1, keepdims=True)
    return (exponent / totals, row_max + jnp.log(totals))


def contract_rows(left, right):
    return lax.dot_general(
        left, right, (((0,), (0,)), ((), ())), preferred_element_type=jnp.float32
    )


def contract_cols(left, right):
    return lax.dot_general(
        left, right, (((1,), (1,)), ((), ())), preferred_element_type=jnp.float32
    )


def shards(
    block_entry_states,
    block_result_cotangent,
    token_assignments,
    packed_segment_sizes,
    admitted_route_quota,
    mixing_scale_factor,
    asker_projection,
    lookup_projection,
    content_projection,
    mixing_projection_back,
    asker_scale_factor,
    lookup_scale_factor,
    specialist_scale_factor,
    dispatcher_projection,
    specialist_switch_tensor,
    specialist_widen_tensor,
    specialist_shrink_tensor,
):
    tokens_dev = block_entry_states.shape[1]
    width = block_entry_states.shape[2]
    halves = lax.axis_size("dp")
    half_index = lax.axis_index("dp")
    row_len = tokens_dev * halves
    heads_local = HEADS // halves
    head_width = width // HEADS
    half_width = width // halves
    score_scale = head_width ** (-0.5)
    lengths = packed_segment_sizes[0]
    row_positions = jnp.arange(row_len, dtype=jnp.int32)
    doc_ids, doc_offset = doc_places(lengths, row_positions)
    allowed = (doc_ids[None, :] == doc_ids[:, None]) & (
        row_positions[None, :] <= row_positions[:, None]
    )
    cos_table, sin_table = rope_tables(doc_offset, head_width)
    head_shape = (row_len, heads_local, head_width)
    column_start = half_index * half_width
    query_half_gain = lax.dynamic_slice_in_dim(asker_scale_factor, column_start, half_width)
    key_half_gain = lax.dynamic_slice_in_dim(lookup_scale_factor, column_start, half_width)
    inputs = block_entry_states[0].astype(jnp.float32)
    factor_in = rms_factor(inputs)
    normed_in = (inputs * factor_in * mixing_scale_factor).astype(jnp.bfloat16)
    query_cols, key_cols, value_cols, output_rows = (
        *sent_together((asker_projection, lookup_projection, content_projection), "expert", 0, 1),
        lax.all_gather(mixing_projection_back, "expert", axis=0, tiled=True),
    )
    normed_full = lax.all_gather(normed_in, "dp", axis=0, tiled=True)
    query_proj = jnp.dot(normed_full, query_cols, preferred_element_type=jnp.float32)
    key_proj = jnp.dot(normed_full, key_cols, preferred_element_type=jnp.float32)
    value_low = (
        jnp.dot(normed_full, value_cols, preferred_element_type=jnp.float32)
        .astype(jnp.bfloat16)
        .reshape(head_shape)
    )
    query_sq, key_sq = lax.psum(
        (jnp.sum(query_proj * query_proj, axis=1), jnp.sum(key_proj * key_proj, axis=1)), "dp"
    )
    query_factor = lax.rsqrt(query_sq[:, None] / width + EPS)
    key_factor = lax.rsqrt(key_sq[:, None] / width + EPS)
    queries = rotate(
        (query_proj * query_factor * query_half_gain).reshape(head_shape), cos_table, sin_table
    ).astype(jnp.bfloat16)
    keys = rotate(
        (key_proj * key_factor * key_half_gain).reshape(head_shape), cos_table, sin_table
    ).astype(jnp.bfloat16)
    raw_scores = (
        jnp.einsum("qhd,khd->hqk", queries, keys, preferred_element_type=jnp.float32) * score_scale
    )
    masked_scores = jnp.where(allowed[None], raw_scores, NEG)
    attn_probs, log_total = softmax_rows(masked_scores)
    attn_low = attn_probs.astype(jnp.bfloat16)
    mixed_heads = (
        jnp.einsum("hqk,khd->qhd", attn_low, value_low, preferred_element_type=jnp.float32)
        .reshape(row_len, half_width)
        .astype(jnp.bfloat16)
    )
    attn_share = jnp.dot(mixed_heads, output_rows, preferred_element_type=jnp.float32)
    attn_own = lax.psum_scatter(
        attn_share.astype(jnp.bfloat16), "dp", scatter_dimension=0, tiled=True
    ).astype(jnp.float32)
    hidden = inputs + attn_own
    factor_moe = rms_factor(hidden)
    normed_moe = (hidden * factor_moe * specialist_scale_factor).astype(jnp.bfloat16)
    experts = dispatcher_projection.shape[1]
    top_routes = token_assignments.shape[2]
    logits = jnp.dot(normed_moe, dispatcher_projection, preferred_element_type=jnp.float32)
    route_probs, unused_total = softmax_rows(logits)
    expert_ids = token_assignments[0].reshape(-1)
    selected_specialists = (
        expert_ids[:, None] == jnp.arange(experts, dtype=jnp.int32)[None, :]
    ).astype(jnp.int32)
    before = jnp.cumsum(selected_specialists, axis=0, dtype=jnp.int32) - selected_specialists
    route_rank = jnp.sum(before * selected_specialists, axis=1, dtype=jnp.int32)
    specialist_slot_ceilings = jnp.sum(
        selected_specialists * admitted_route_quota[None, :], axis=1, dtype=jnp.int32
    )
    kept_mask = route_rank < specialist_slot_ceilings
    kept_float = kept_mask.astype(jnp.float32)
    sent_counts = jnp.sum(
        selected_specialists * kept_mask[:, None].astype(jnp.int32), axis=0, dtype=jnp.int32
    )
    capacity = 3 * tokens_dev * top_routes // (4 * experts)
    total_slots = experts * capacity
    local_experts = specialist_switch_tensor.shape[0]
    sources = experts // local_experts
    slot_index = jnp.where(kept_mask, expert_ids * capacity + route_rank, total_slots)
    slot_clip = jnp.minimum(slot_index, total_slots - 1)
    token_owner = jnp.arange(tokens_dev * top_routes, dtype=jnp.int32) // top_routes
    picked_float = selected_specialists.astype(jnp.float32).reshape(tokens_dev, top_routes, experts)
    gate_value = jnp.sum(picked_float * route_probs[:, None, :], axis=2) * kept_float.reshape(
        tokens_dev, top_routes
    )
    send_rows = (
        jnp.zeros((total_slots, width), jnp.bfloat16)
        .at[slot_index]
        .set(normed_moe[token_owner], mode="drop")
    )
    send_rows = send_rows.reshape(sources, local_experts, capacity, width)
    got_counts = lax.all_to_all(
        sent_counts.reshape(sources, local_experts),
        "expert",
        split_axis=0,
        concat_axis=0,
        tiled=True,
    )
    gate_part = specialist_switch_tensor[0]
    up_part = specialist_widen_tensor[0]
    down_part = specialist_shrink_tensor[0]

    def expert_forward(rows_in):
        gate_in = jnp.einsum(
            "secd,df->secf", rows_in, gate_part, preferred_element_type=jnp.float32
        )
        up_in = jnp.einsum("secd,df->secf", rows_in, up_part, preferred_element_type=jnp.float32)
        active_rows = (gate_in * jax.nn.sigmoid(gate_in) * up_in).astype(jnp.bfloat16)
        result = jnp.einsum(
            "secf,fd->secd", active_rows, down_part, preferred_element_type=jnp.float32
        ).astype(jnp.bfloat16)
        return (result, gate_in, up_in, rows_in)

    expert_out, gate_pre, up_pre, arrived = grouped_exchange(
        send_rows, "expert", 0, 0, expert_forward, 2, 2
    )
    returned = lax.all_to_all(
        expert_out, "expert", split_axis=0, concat_axis=0, tiled=True
    ).reshape(total_slots, width)
    route_out = returned[slot_clip].astype(jnp.float32).reshape(tokens_dev, top_routes, width)
    moe_part = jnp.sum(gate_value[:, :, None] * route_out, axis=1)
    block_output = hidden + moe_part
    grad_top = block_result_cotangent[0].astype(jnp.float32)
    gate_grad = jnp.sum(route_out * grad_top[:, None, :], axis=2) * kept_float.reshape(
        tokens_dev, top_routes
    )
    route_grad = (
        (gate_value[:, :, None] * grad_top[:, None, :])
        .astype(jnp.bfloat16)
        .reshape(tokens_dev * top_routes, width)
    )
    send_grads = (
        jnp.zeros((total_slots, width), jnp.bfloat16).at[slot_index].set(route_grad, mode="drop")
    )
    send_grads = send_grads.reshape(sources, local_experts, capacity, width)
    arrived_grads = lax.all_to_all(send_grads, "expert", split_axis=0, concat_axis=0, tiled=True)
    act_grad = jnp.einsum(
        "secd,fd->secf", arrived_grads, down_part, preferred_element_type=jnp.float32
    )
    sigmoid_gate = jax.nn.sigmoid(gate_pre)
    silu_gate = gate_pre * sigmoid_gate
    activation = (silu_gate * up_pre).astype(jnp.bfloat16)
    gate_pre_grad = (
        act_grad * up_pre * sigmoid_gate * (1.0 + gate_pre * (1.0 - sigmoid_gate))
    ).astype(jnp.bfloat16)
    up_pre_grad = (act_grad * silu_gate).astype(jnp.bfloat16)
    down_grad_local = jnp.einsum(
        "secf,secd->fd", activation, arrived_grads, preferred_element_type=jnp.float32
    )
    gate_grad_local = jnp.einsum(
        "secf,secd->fd", gate_pre_grad, arrived, preferred_element_type=jnp.float32
    )
    up_grad_local = jnp.einsum(
        "secf,secd->fd", up_pre_grad, arrived, preferred_element_type=jnp.float32
    )
    row_terms = jnp.einsum(
        "secf,df->secd", gate_pre_grad, gate_part, preferred_element_type=jnp.float32
    ) + jnp.einsum("secf,df->secd", up_pre_grad, up_part, preferred_element_type=jnp.float32)
    row_grad = row_terms.astype(jnp.bfloat16)
    returned_grads = lax.all_to_all(
        row_grad, "expert", split_axis=0, concat_axis=0, tiled=True
    ).reshape(total_slots, width)
    route_back = returned_grads[slot_clip].astype(jnp.float32) * kept_float[:, None]
    moe_in_grad = jnp.sum(route_back.reshape(tokens_dev, top_routes, width), axis=1)
    prob_grad = jnp.sum(picked_float * gate_grad[:, :, None], axis=1)
    logit_grad = (
        route_probs * (prob_grad - jnp.sum(route_probs * prob_grad, axis=1, keepdims=True))
    ).astype(jnp.bfloat16)
    router_grad_local = contract_rows(normed_moe, logit_grad)
    moe_in_grad = moe_in_grad + contract_cols(logit_grad, dispatcher_projection)
    hidden_norm_grad, moe_gain_local = norm_back(
        moe_in_grad, hidden, factor_moe, specialist_scale_factor
    )
    hidden_grad = grad_top + hidden_norm_grad
    hidden_low = hidden_grad.astype(jnp.bfloat16)
    grad_full = lax.all_gather(hidden_low, "dp", axis=0, tiled=True)
    mixed_grad = contract_cols(grad_full, output_rows).astype(jnp.bfloat16).reshape(head_shape)
    again_scores = (
        jnp.einsum("qhd,khd->hqk", queries, keys, preferred_element_type=jnp.float32) * score_scale
    )
    back_probs = jnp.exp(jnp.where(allowed[None], again_scores, NEG) - log_total)
    back_low = back_probs.astype(jnp.bfloat16)
    prob_grad_att = jnp.einsum(
        "qhd,khd->hqk", mixed_grad, value_low, preferred_element_type=jnp.float32
    )
    score_grad = (
        back_probs * (prob_grad_att - jnp.sum(back_probs * prob_grad_att, axis=-1, keepdims=True))
    ).astype(jnp.bfloat16)
    query_rot_grad = (
        jnp.einsum("hqk,khd->qhd", score_grad, keys, preferred_element_type=jnp.float32)
        * score_scale
    )
    key_rot_grad = (
        jnp.einsum("hqk,qhd->khd", score_grad, queries, preferred_element_type=jnp.float32)
        * score_scale
    )
    value_grad = jnp.einsum(
        "hqk,qhd->khd", back_low, mixed_grad, preferred_element_type=jnp.float32
    )
    query_norm_grad = unrotate(query_rot_grad, cos_table, sin_table).reshape(row_len, half_width)
    key_norm_grad = unrotate(key_rot_grad, cos_table, sin_table).reshape(row_len, half_width)
    query_scaled = query_norm_grad * query_half_gain
    key_scaled = key_norm_grad * key_half_gain
    query_inner, key_inner = lax.psum(
        (jnp.sum(query_scaled * query_proj, axis=1), jnp.sum(key_scaled * key_proj, axis=1)), "dp"
    )
    query_proj_grad = query_factor * (
        query_scaled - query_proj * query_factor * query_factor * (query_inner[:, None] / width)
    )
    key_proj_grad = key_factor * (
        key_scaled - key_proj * key_factor * key_factor * (key_inner[:, None] / width)
    )
    empty_gain = jnp.zeros((width,), jnp.float32)
    query_gain_local = lax.dynamic_update_slice_in_dim(
        empty_gain, jnp.sum(query_norm_grad * query_proj * query_factor, axis=0), column_start, 0
    )
    key_gain_local = lax.dynamic_update_slice_in_dim(
        empty_gain, jnp.sum(key_norm_grad * key_proj * key_factor, axis=0), column_start, 0
    )
    query_low = query_proj_grad.astype(jnp.bfloat16)
    key_low = key_proj_grad.astype(jnp.bfloat16)
    value_proj_low = value_grad.reshape(row_len, half_width).astype(jnp.bfloat16)
    normed_in_share = (
        contract_cols(query_low, query_cols)
        + contract_cols(key_low, key_cols)
        + contract_cols(value_proj_low, value_cols)
    )
    normed_in_grad, gate_units, up_units, down_weight_grad = (
        lax.psum_scatter(
            normed_in_share.astype(jnp.bfloat16), "dp", scatter_dimension=0, tiled=True
        ).astype(jnp.float32),
        *tuple(
            (
                part.astype(jnp.float32)
                for part in sent_together_2(
                    (
                        gate_grad_local.astype(jnp.bfloat16),
                        up_grad_local.astype(jnp.bfloat16),
                        down_grad_local.astype(jnp.bfloat16),
                    ),
                    "dp",
                    0,
                    1,
                )
            )
        ),
    )
    gate_weight_grad = gate_units.T
    up_weight_grad = up_units.T
    input_norm_grad, attn_gain_local = norm_back(
        normed_in_grad, inputs, factor_in, mixing_scale_factor
    )
    input_grad = hidden_grad + input_norm_grad
    rows_dev = width // lax.axis_size("expert")
    out_part = contract_rows(mixed_heads, grad_full).reshape(
        lax.axis_size("expert") * rows_dev, half_width
    )
    shares = lax.psum_scatter(
        jnp.concatenate(
            [
                contract_rows(normed_full, query_low),
                contract_rows(normed_full, key_low),
                contract_rows(normed_full, value_proj_low),
                out_part,
            ],
            axis=1,
        ),
        "expert",
        scatter_dimension=0,
        tiled=True,
    )
    gain_sums, router_weight_grad = in_one(
        (
            jnp.stack([attn_gain_local, query_gain_local, key_gain_local, moe_gain_local]),
            router_grad_local,
        ),
        ("dp", "expert"),
    )
    output_grad_rows = shares[:, 3 * half_width :].reshape(rows_dev // 2, width)
    return (
        block_output[None],
        input_grad[None],
        gain_sums[0],
        shares[:, :half_width],
        shares[:, half_width : 2 * half_width],
        shares[:, 2 * half_width : 3 * half_width],
        output_grad_rows,
        gain_sums[1],
        gain_sums[2],
        gain_sums[3],
        router_weight_grad,
        gate_weight_grad[None],
        up_weight_grad[None],
        down_weight_grad[None],
        got_counts.T,
    )


def solution(mesh):
    placed = (
        P("expert", "dp", None),
        P("expert", "dp", None),
        P("expert", "dp", None),
        P("expert", None),
        P(),
        P(),
        P("expert", "dp"),
        P("expert", "dp"),
        P("expert", "dp"),
        P(("dp", "expert"), None),
        P(),
        P(),
        P(),
        P(),
        P("expert", None, None),
        P("expert", None, None),
        P("expert", None, None),
    )
    return jax.shard_map(
        shards,
        mesh=mesh,
        in_specs=placed,
        out_specs=(
            P("expert", "dp", None),
            P("expert", "dp", None),
            P(),
            P("expert", "dp"),
            P("expert", "dp"),
            P("expert", "dp"),
            P(("dp", "expert"), None),
            P(),
            P(),
            P(),
            P(),
            P("expert", None, "dp"),
            P("expert", None, "dp"),
            P("expert", "dp", None),
            P("expert", "dp"),
        ),
        check_vma=False,
    )
```

profile of v0, /device:TPU:0, one launch (start us, length us, event | category | flops | bytes accessed | tf_op | source)
XLA Modules:
  0.0 1211.9 jit_solution(13122846190038920725)
XLA Ops:
  25.5 95.8 %all-gather.7.cloned.1.call-done = bf16[2048,3072]{1,0:T(8,128)(2,1)} async-done(((bf16[32,3072]{1,0:T(8,128)(2,1)}), bf16[2048,3072]{1,0:T(8,128)(2,1)}) %all-gather.7.cloned.1.call-update) | async-done | bytes 12582928 | tf_op jit(solution)/shard_map/all_gather | solution.py:17
  142.2 50.6 %all-gather.9.cloned.1.call-done = bf16[1024,2048]{1,0:T(8,128)(2,1)} async-done(((bf16[16,2048]{1,0:T(8,128)(2,1)}), bf16[1024,2048]{1,0:T(8,128)(2,1)}) %all-gather.9.cloned.1.call-update) | async-done | bytes 4194320 | tf_op jit(solution)/shard_map/all_gather | solution.py:165
  197.8 18.2 %reduce-window.19 = s32[64,8,128]{2,1,0:T(8,128)S(1)} reduce-window(s32[64,8,128]{2,1,0:T(8,128)S(1)} %fusion.115, s32[]{:T(128)} %constant.68.clone.1), window={size=1x1x128 pad=0_0x0_0x127_0}, to_apply=%region_11.12 | reduce-window | flops 8323072 | bytes 524292 | tf_op jit(solution)/shard_map/reduce-window.1
  221.9 21.3 %scatter_custom_fusion = bf16[768,2048]{1,0:T(8,128)(2,1)S(1)} fusion(s32[1024]{0:T(1024)} %bitcast.278, bf16[128,2048]{1,0:T(8,128)(2,1)} %multiply_convert_fusion.9, s32[1024]{0:T(1024)} %broadcast_clamp_fusion.1, bf16[]{:T(256)} %constant.78.clone.1), kind=kCustom, calls=%fused_computation.38 | custom fusion | bytes 3146240 | tf_op jit(solution)/shard_map/scatter | solution.py:236
  259.9 28.2 %all-to-all-done.1 = bf16[64,1,6,2048]{3,2,1,0:T(8,128)(2,1)S(1)} async-done(((bf16[64,1,6,2048]{3,2,1,0:T(8,128)(2,1)}), bf16[64,1,6,2048]{3,2,1,0:T(8,128)(2,1)S(1)}, u32[]{:S(2)}, u32[]{:S(2)}) %all-to-all-start.1) | async-done | bytes 1572896 | tf_op jit(solution)/shard_map/all_to_all | solution.py:34
  296.2 8.3 scatter_custom_fusion.1
  314.1 9.4 all-to-all-done
  350.7 31.9 %all-to-all-done.3 = bf16[64,1,12,2048]{3,2,1,0:T(8,128)(2,1)} async-done(((bf16[64,1,12,2048]{3,2,1,0:T(8,128)(2,1)}), bf16[64,1,12,2048]{3,2,1,0:T(8,128)(2,1)}, u32[]{:S(2)}, u32[]{:S(2)}) %all-to-all-start.3) | async-done | bytes 3145760 | tf_op jit(solution)/shard_map/all_to_all | solution.py:283
  382.6 9.0 all-to-all-start.2
  391.7 10.7 multiply_convert_fusion.2
  415.4 29.2 %all-to-all-done.2 = bf16[64,1,12,2048]{3,2,1,0:T(8,128)(2,1)} async-done(((bf16[64,1,12,2048]{3,2,1,0:T(8,128)(2,1)}), bf16[64,1,12,2048]{3,2,1,0:T(8,128)(2,1)}, u32[]{:S(2)}, u32[]{:S(2)}) %all-to-all-start.2) | async-done | bytes 3145760 | tf_op jit(solution)/shard_map/all_to_all | solution.py:264
  444.6 8.7 all-to-all-start.4
  473.0 35.2 %all-to-all-done.4 = bf16[64,1,12,2048]{3,2,1,0:T(8,128)(2,1)} async-done(((bf16[64,1,12,2048]{3,2,1,0:T(8,128)(2,1)}), bf16[64,1,12,2048]{3,2,1,0:T(8,128)(2,1)}, u32[]{:S(2)}, u32[]{:S(2)}) %all-to-all-start.4) | async-done | bytes 3145760 | tf_op jit(solution)/shard_map/all_to_all | solution.py:307
  578.9 13.1 %bitcast_convert_fusion = bf16[1024,2048]{1,0:T(8,128)(2,1)} fusion(bf16[64,1,12,2048]{3,2,1,0:T(8,128)(2,1)} %all-to-all-done.3, f32[64,6,1024]{2,0,1:T(8,128)S(1)} %copy-done.99, f32[64,6,1024]{2,0,1:T(8,128)S(1)} %copy-done.104, f32[64,6,1024]{2,0,1:T(8,128)S(1)} %copy-done.102, f32[64,6,1024]{2,0,1:T(8,128)S(1)} %copy-done.106), kind=kOutput, calls=%fused_computation.13 | convolution fusion | flops 3229614080 | bytes 13631488 | tf_op jit(solution)/shard_map/secf,secd->fd/dot_general | solution.py:294
  595.1 11.0 pad_maximum_fusion.1
  612.0 9.4 reshape.623
  621.4 9.4 copy.270
  634.6 15.1 %pad_maximum_fusion = f32[2048,4096]{0,1:T(8,128)} fusion(f32[2048,1024]{0,1:T(8,128)} %copy.270, f32[2048,1024]{0,1:T(8,128)S(1)} %fusion.139, f32[2048,1024]{0,1:T(8,128)S(1)} %fusion.137, f32[2048,1024]{0,1:T(8,128)S(1)} %fusion.136), kind=kLoop, calls=%fused_computation.5 | loop fusion | flops 25165824 | bytes 67108864 | tf_op jit(solution)/shard_map/concatenate | solution.py:406
  649.7 31.1 %copy.290 = f32[2048,4096]{1,0:T(8,128)} copy(f32[2048,4096]{0,1:T(8,128)} %pad_maximum_fusion) | data formatting | bytes 67108864
  681.7 19.8 %all_to_all.34 = s32[64,1,1]{2,1,0:T(1,128)S(1)} all-to-all(s32[64,1,1]{2,1,0:T(1,128)S(1)} %copy.274), channel_id=1, replica_groups=mesh['dp'=2,'expert'=64] {'expert'}, dimensions={0} | all-to-all | bytes 512 | tf_op jit(solution)/shard_map/all_to_all | solution.py:239
  706.7 35.4 %all-reduce.4.cloned.1.call-done = f32[139264]{0:T(1024)} async-done(((f32[139264]{0:T(1024)}), f32[139264]{0:T(1024)}) %all-reduce.4.cloned.1.call-update) | async-done | bytes 557072 | tf_op jit(solution)/shard_map/psum | solution.py:51
  745.8 21.4 %reduce-scatter.11.cloned.1.call-done = bf16[512,6144]{1,0:T(8,128)(2,1)} async-done(((bf16[1024,6144]{1,0:T(8,128)(2,1)}), bf16[512,6144]{1,0:T(8,128)(2,1)}) %reduce-scatter.11.cloned.1.call-update) | async-done | bytes 6291472 | tf_op jit(solution)/shard_map/reduce_scatter | solution.py:45
  767.2 8.1 fusion.69
  786.0 416.4 %reduce-scatter.13.cloned.1.call-done = f32[32,4096]{1,0:T(8,128)} async-done(((f32[2048,4096]{1,0:T(8,128)}), f32[32,4096]{1,0:T(8,128)}) %reduce-scatter.13.cloned.1.call-update) | async-done | bytes 524304
  (383 shorter events, 249.6 us)
Async XLA Ops:
  7.2 287.5 %copy-start = (bf16[2048,64]{0,1:T(8,128)(2,1)S(1)}, bf16[2048,64]{0,1:T(8,128)(2,1)}, u32[]{:S(2)}) copy-start(bf16[2048,64]{0,1:T(8,128)(2,1)} %param.30) | copy-start | bytes 786436
  7.2 18.3 %all-gather.5.cloned.1.call-start = ((), (), s32[]{:S(2)}) async-start(), calls=%async_computation.10 | async-start | bytes 1572864 | tf_op jit(solution)/shard_map/all_gather | solution.py:167
  11.1 110.1 %all-gather.7.cloned.1.call-start = ((), (), s32[]{:S(2)}) async-start(), calls=%async_computation.11 | async-start | bytes 12779520 | tf_op jit(solution)/shard_map/all_gather | solution.py:17
  12.8 180.0 %all-gather.9.cloned.1.call-start = ((), (), s32[]{:S(2)}) async-start(), calls=%async_computation.12 | async-start | bytes 4259840 | tf_op jit(solution)/shard_map/all_gather | solution.py:165
  13.5 205.0 %reduce-scatter.7.cloned.1.call-start = ((), (), s32[]{:S(2)}) async-start(), calls=%async_computation.13 | async-start | bytes 1572864 | tf_op jit(solution)/shard_map/reduce_scatter | solution.py:198
  15.1 118.0 %copy-start.57 = (f32[1024]{0:T(1024)}, f32[1024]{0:T(1024)S(1)}, u32[]{:S(2)}) copy-start(f32[1024]{0:T(1024)S(1)} %dynamic_slice.6) | copy-start | bytes 12292
  15.8 116.9 %copy-start.59 = (f32[1024]{0:T(1024)}, f32[1024]{0:T(1024)S(1)}, u32[]{:S(2)}) copy-start(f32[1024]{0:T(1024)S(1)} %dynamic_slice.7) | copy-start | bytes 12292
  25.5 99.6 %copy-start.8 = (bf16[256,2048]{1,0:T(8,128)(2,1)S(1)}, bf16[256,2048]{1,0:T(8,128)(2,1)}, u32[]{:S(2)}) copy-start(bf16[256,2048]{1,0:T(8,128)(2,1)} %all-gather.5.cloned.1.call-done) | copy-start | bytes 3145732
  142.1 50.6 %copy-start.44 = (bf16[8,128,256]{2,1,0:T(8,128)(2,1)}, bf16[8,128,256]{2,1,0:T(8,128)(2,1)S(1)}, u32[]{:S(2)}) copy-start(bf16[8,128,256]{2,1,0:T(8,128)(2,1)S(1)} %convolution_convert_fusion.2) | copy-start | bytes 1572868
  251.8 36.3 %all-to-all-start.1 = ((bf16[64,1,6,2048]{3,2,1,0:T(8,128)(2,1)}), bf16[64,1,6,2048]{3,2,1,0:T(8,128)(2,1)S(1)}, u32[]{:S(2)}, u32[]{:S(2)}) async-start(bf16[64,1,6,2048]{3,2,1,0:T(8,128)(2,1)} %get-tuple-element.133), calls=%async_computation.2 | async-start | bytes 4194304 | tf_op jit(solution)/shard_map/all_to_all | solution.py:34
  288.1 35.4 %all-to-all-start = ((bf16[64,1,6,2048]{3,2,1,0:T(8,128)(2,1)}), bf16[64,1,6,2048]{3,2,1,0:T(8,128)(2,1)}, u32[]{:S(2)}, u32[]{:S(2)}) async-start(bf16[64,1,6,2048]{3,2,1,0:T(8,128)(2,1)} %get-tuple-element.132), calls=%async_computation.1 | async-start | bytes 4194304 | tf_op jit(solution)/shard_map/all_to_all | solution.py:34
  314.1 77.5 %copy-start.98 = (f32[64,6,1024]{2,0,1:T(8,128)}, f32[64,6,1024]{2,0,1:T(8,128)S(1)}, u32[]{:S(2)}) copy-start(f32[64,6,1024]{2,0,1:T(8,128)S(1)} %fusion.14) | copy-start | bytes 4718596
  323.5 59.1 %all-to-all-start.3 = ((bf16[64,1,12,2048]{3,2,1,0:T(8,128)(2,1)}), bf16[64,1,12,2048]{3,2,1,0:T(8,128)(2,1)}, u32[]{:S(2)}, u32[]{:S(2)}) async-start(bf16[64,1,12,2048]{3,2,1,0:T(8,128)(2,1)} %bitcast.256), calls=%async_computation.4 | async-start | bytes 8388608 | tf_op jit(solution)/shard_map/all_to_all | solution.py:283
  350.7 41.0 %copy-start.101 = (f32[64,6,1024]{2,0,1:T(8,128)S(1)}, f32[64,6,1024]{2,0,1:T(8,128)}, u32[]{:S(2)}) copy-start(f32[64,6,1024]{2,0,1:T(8,128)} %copy-done.100) | copy-start | bytes 4718596
  382.6 62.0 %all-to-all-start.2 = ((bf16[64,1,12,2048]{3,2,1,0:T(8,128)(2,1)}), bf16[64,1,12,2048]{3,2,1,0:T(8,128)(2,1)}, u32[]{:S(2)}, u32[]{:S(2)}) async-start(bf16[64,1,12,2048]{3,2,1,0:T(8,128)(2,1)} %copy.250), calls=%async_computation.3 | async-start | bytes 8388608 | tf_op jit(solution)/shard_map/all_to_all | solution.py:264
  415.4 39.2 %copy-start.69 = (f32[8,256]{1,0:T(8,128)S(1)}, f32[8,256]{1,0:T(8,128)}, u32[]{:S(2)}) copy-start(f32[8,256]{1,0:T(8,128)} %copy-done.68) | copy-start | bytes 24580
  415.4 39.8 %copy-start.67 = (f32[128,8]{0,1:T(8,128)S(1)}, f32[128,8]{0,1:T(8,128)}, u32[]{:S(2)}) copy-start(f32[128,8]{0,1:T(8,128)} %copy-done.66) | copy-start | bytes 12292
  444.6 63.5 %all-to-all-start.4 = ((bf16[64,1,12,2048]{3,2,1,0:T(8,128)(2,1)}), bf16[64,1,12,2048]{3,2,1,0:T(8,128)(2,1)}, u32[]{:S(2)}, u32[]{:S(2)}) async-start(bf16[64,1,12,2048]{3,2,1,0:T(8,128)(2,1)} %copy.254), calls=%async_computation.5 | async-start | bytes 8388608 | tf_op jit(solution)/shard_map/all_to_all | solution.py:307
  453.3 86.1 %all-gather.11.cloned.1.call-start = ((), (), s32[]{:S(2)}) async-start(), calls=%async_computation.14 | async-start | bytes 1572864 | tf_op jit(solution)/shard_map/all_gather | solution.py:323
  529.3 63.4 %reduce-scatter.9.cloned.1.call-start = ((), (), s32[]{:S(2)}) async-start(), calls=%async_computation.15 | async-start | bytes 1572864 | tf_op jit(solution)/shard_map/reduce_scatter | solution.py:376
  570.8 171.2 %all-reduce.4.cloned.1.call-start = ((), (), s32[]{:S(2)}) async-start(), calls=%async_computation.16 | async-start | bytes 1114112 | tf_op jit(solution)/shard_map/psum | solution.py:51
  595.0 172.2 %reduce-scatter.11.cloned.1.call-start = ((), (), s32[]{:S(2)}) async-start(), calls=%async_computation.17 | async-start | bytes 18874368 | tf_op jit(solution)/shard_map/reduce_scatter | solution.py:45
  606.1 596.3 %reduce-scatter.13.cloned.1.call-start = ((), (), s32[]{:S(2)}) async-start(), calls=%async_computation.18 | async-start | bytes 34078720
  780.7 424.3 %copy-start.1 = (bf16[2048,64]{0,1:T(8,128)(2,1)S(1)}, bf16[2048,64]{0,1:T(8,128)(2,1)}, u32[]{:S(2)}) copy-start(bf16[2048,64]{0,1:T(8,128)(2,1)} %param.30) | copy-start | bytes 786436
  (98 other events, 709.8 us)
Sparse Core Ops, SparseCore 0:
  11.3 14.1 all-gather.4
  28.8 92.4 all-gather.6
  124.1 68.5 all-gather.8
  197.4 8.5 reduce-scatter.6
  529.4 9.9 all-gather.10
  570.9 12.4 reduce-scatter.8
  595.2 146.8 all-reduce.3
  744.6 22.5 reduce-scatter.10
  769.7 432.6 reduce-scatter.12
where the time goes:
time: 1220 us; the launch traced here: 1210 us
  waiting for transfers between devices  764 us (63%)
  local copies, waits for them, and re-layouts  150 us (12%)
  matrix products  112 us (9%)
  other arithmetic  107 us (9%)
  starting transfers between devices  38.2 us (3%)
  blocking collectives  25.5 us (2%)
  between operations  15.8 us (1%)
    unnamed x10, waiting for transfers between devices  417 us
    all_gather x1, waiting for transfers between devices, sent_together(): whole = lax.all_gather(both, axis, axis=dim, tiled=True)  95.8 us
    unnamed x224, local copies, waits for them, and re-layouts  53.9 us
    all_gather x1, waiting for transfers between devices, shards(): lax.all_gather(mixing_projection_back, 'expert', axis=0, tiled=True)  50.6 us
    all_to_all x2, waiting for transfers between devices, grouped_exchange(): lax.all_to_all(group, axis, split_axis=split_dim, concat_axis=concat_dim,...  37.6 us
    psum x1, waiting for transfers between devices, in_one(): so_far = lax.psum(ravelled, axis)  35.4 us
    all_to_all x1, waiting for transfers between devices, shards(): lax.all_to_all(row_grad, 'expert', split_axis=0, concat_axis=0, tiled=True)  35.2 us
    all_to_all x1, waiting for transfers between devices, shards(): lax.all_to_all(send_grads, 'expert', split_axis=0, concat_axis=0, tiled=T...  31.9 us
  transfers between devices with their start and end apart: 14, of which 12 were waited for; matrix products, arithmetic and copies ran while one was open for 22% of the time, Pallas kernels for 0%

commit v1 on v0

v1 whole, which is shorter than its diff:
```python
import jax
import jax.numpy as jnp
from jax import lax
from jax.experimental import pallas as pl
from jax.experimental.pallas import tpu as pltpu
from jax.sharding import PartitionSpec as P

HEADS = 16
EPS = 1e-05
THETA = 10000.0
NEG = -1e30
BOTH = ("dp", "expert")

FLIPS = ((1, 4, 16), (3, 12, 48))
STEPS = 6


def flip_of(core, part, step):
    return FLIPS[core][step] if step < 3 else FLIPS[1 - core][(step + part) % 3]


def mask_of(core, part, index):
    mask = 0
    for step in range(STEPS):
        if (index >> step) & 1:
            mask ^= flip_of(core, part, step)
    return mask


def permute_step(value, part, step):
    pairs = []
    for core in range(2):
        flip = flip_of(core, part, step)
        pairs += [(64 * core + d, 64 * core + (d ^ flip)) for d in range(64)]
    return lax.ppermute(value, BOTH, pairs)


def relative_order(core, me, part):
    tables = [jnp.array([mask_of(c, part, r) for r in range(64)], jnp.int32) for c in range(2)]
    return jnp.where(core == 0, tables[0], tables[1]) ^ me


def natural_order(order):
    return jnp.argmax(order[None, :] == jnp.arange(64, dtype=jnp.int32)[:, None], axis=1)


def reorder(rows, order):
    blocks = rows.reshape(64, rows.shape[0] // 64, rows.shape[1])
    return jnp.take(blocks, order, axis=0, mode="clip").reshape(rows.shape)


def sum_everywhere(rows, core, part):
    half = rows.shape[1] // 2
    own = lax.dynamic_slice_in_dim(rows, core * half, half, axis=1)
    own = own + swap(lax.dynamic_slice_in_dim(rows, (1 - core) * half, half, axis=1))
    for step in range(STEPS):
        own = own + permute_step(own, part, step)
    other = swap(own)
    return jnp.concatenate(
        [jnp.where(core == 0, own, other), jnp.where(core == 0, other, own)], axis=1
    )


def swap(value):
    return lax.ppermute(value, "dp", [(0, 1), (1, 0)])


def dot(left, right):
    return jnp.dot(left, right, preferred_element_type=jnp.float32)


def dot_tn(left, right):
    return lax.dot_general(
        left, right, (((0,), (0,)), ((), ())), preferred_element_type=jnp.float32
    )


def dot_nt(left, right):
    return lax.dot_general(
        left, right, (((1,), (1,)), ((), ())), preferred_element_type=jnp.float32
    )


def rms_factor(values):
    return lax.rsqrt(jnp.mean(values * values, axis=-1, keepdims=True) + EPS)


def norm_back(grad_normed, source, factor, gain):
    scaled = grad_normed * gain
    grad_source = factor * (
        scaled - source * factor * factor * jnp.mean(scaled * source, axis=-1, keepdims=True)
    )
    grad_gain = jnp.sum(grad_normed * source * factor, axis=0)
    return (grad_source, grad_gain)


def doc_places(lengths, places):
    ends = jnp.cumsum(lengths, dtype=jnp.int32)
    done = ends[None, :] <= places[:, None]
    doc_ids = jnp.sum(done.astype(jnp.int32), axis=1, dtype=jnp.int32)
    starts = jnp.sum(jnp.where(done, lengths[None, :], 0), axis=1, dtype=jnp.int32)
    return (doc_ids, places - starts)


def rope_tables(offsets, head_width):
    half_width = head_width // 2
    inverse = THETA ** (-jnp.arange(half_width, dtype=jnp.float32) * 2.0 / head_width)
    angles = offsets.astype(jnp.float32)[..., None] * inverse
    return (jnp.cos(angles)[..., None, :], jnp.sin(angles)[..., None, :])


def rotate(values, cos_table, sin_table):
    half_width = values.shape[-1] // 2
    first, second = (values[..., :half_width], values[..., half_width:])
    return jnp.concatenate(
        [first * cos_table - second * sin_table, second * cos_table + first * sin_table], axis=-1
    )


def unrotate(grads, cos_table, sin_table):
    half_width = grads.shape[-1] // 2
    first, second = (grads[..., :half_width], grads[..., half_width:])
    return jnp.concatenate(
        [first * cos_table + second * sin_table, second * cos_table - first * sin_table], axis=-1
    )


def softmax_rows(values):
    exponent = jnp.exp(values - jnp.max(values, axis=-1, keepdims=True))
    return exponent / jnp.sum(exponent, axis=-1, keepdims=True)


def half_picker(count, half):
    rows = lax.broadcasted_iota(jnp.int32, (count // 2, count), 0)
    cols = lax.broadcasted_iota(jnp.int32, (count // 2, count), 1)
    return (cols == 2 * rows + half).astype(jnp.float32).astype(jnp.bfloat16)


def unpack_block(packed):
    count, width = packed.shape[0], packed.shape[1] * 2 // 3
    spare = packed[:, width:]
    rest = [dot(half_picker(count, h), spare).astype(jnp.bfloat16) for h in range(2)]
    return packed[:, :width], rest


def pack_block(rows, out_ref):
    count, width = out_ref.shape[0], rows.shape[1]
    half = width // 2
    out_ref[:, :width] = rows[:count]
    out_ref[:, width:] = (
        dot_tn(half_picker(count, 0), rows[count:, :half])
        + dot_tn(half_picker(count, 1), rows[count:, half:])
    ).astype(jnp.bfloat16)


def unpack_body(packed_ref, rows_ref):
    main, rest = unpack_block(packed_ref[...])
    count, width = main.shape
    rows_ref[:count] = main
    rows_ref[count:, : width // 2] = rest[0]
    rows_ref[count:, width // 2 :] = rest[1]


def unpack(packed):
    count, width = packed.shape[0], packed.shape[1] * 2 // 3
    block = count // 2
    return pl.pallas_call(
        unpack_body,
        grid=(2,),
        in_specs=[pl.BlockSpec((block, width * 3 // 2), lambda i: (i, 0))],
        out_specs=pl.BlockSpec((block * 3 // 2, width), lambda i: (i, 0)),
        out_shape=jax.ShapeDtypeStruct((count * 3 // 2, width), jnp.bfloat16),
        compiler_params=pltpu.CompilerParams(vmem_limit_bytes=32 * 1024 * 1024),
    )(packed)


def send_body(main_ref, spare_ref, rows_ref, out_ref):
    width = rows_ref.shape[1]
    half, count = width // 2, rows_ref.shape[0]
    out_ref[:, :width] = dot_tn(main_ref[...], rows_ref[...]).astype(jnp.bfloat16)
    out_ref[:, width:] = (
        dot_tn(spare_ref[:count], rows_ref[:, :half])
        + dot_tn(spare_ref[count:], rows_ref[:, half:])
    ).astype(jnp.bfloat16)


def to_experts(main, spare, rows):
    tokens, lines = main.shape
    width, block = rows.shape[1], lines // 2
    return pl.pallas_call(
        send_body,
        grid=(2,),
        in_specs=[
            pl.BlockSpec((tokens, block), lambda i: (0, i)),
            pl.BlockSpec((2 * tokens, block), lambda i: (0, i)),
            pl.BlockSpec((tokens, width), lambda i: (0, 0)),
        ],
        out_specs=pl.BlockSpec((block, width * 3 // 2), lambda i: (i, 0)),
        out_shape=jax.ShapeDtypeStruct((lines, width * 3 // 2), jnp.bfloat16),
        compiler_params=pltpu.CompilerParams(vmem_limit_bytes=32 * 1024 * 1024),
    )(main, spare, rows)


def combine_body(main_ref, spare_ref, lines_ref, out_ref):
    tokens, width = out_ref.shape
    half = width // 2
    spare_lines = lines_ref[:, width:]
    out_ref[:, :half] = dot(main_ref[...], lines_ref[:, :half]) + dot(
        spare_ref[:tokens], spare_lines
    )
    out_ref[:, half:] = dot(main_ref[...], lines_ref[:, half:width]) + dot(
        spare_ref[tokens:], spare_lines
    )


def from_experts(main, spare, lines):
    return pl.pallas_call(
        combine_body,
        out_shape=jax.ShapeDtypeStruct((main.shape[0], lines.shape[1] * 2 // 3), jnp.float32),
        compiler_params=pltpu.CompilerParams(vmem_limit_bytes=32 * 1024 * 1024),
    )(main, spare, lines)


def out_body(core_ref, act_ref, own_ref, other_ref, out_ref):
    rows = dot(act_ref[0], own_ref[...]) + dot(act_ref[1], other_ref[...])
    pack_block(rows.astype(jnp.bfloat16), out_ref)


def expert_results(acts, down_w, core):
    _, count, units = acts.shape
    width, block = down_w.shape[1], count // 2
    return pl.pallas_call(
        out_body,
        grid_spec=pltpu.PrefetchScalarGridSpec(
            num_scalar_prefetch=1,
            grid=(2,),
            in_specs=[
                pl.BlockSpec((2, block, units), lambda i, c: (0, i, 0)),
                pl.BlockSpec((units, width), lambda i, c: (c[0], 0)),
                pl.BlockSpec((units, width), lambda i, c: (1 - c[0], 0)),
            ],
            out_specs=pl.BlockSpec((block * 2 // 3, width * 3 // 2), lambda i, c: (i, 0)),
        ),
        out_shape=jax.ShapeDtypeStruct((count * 2 // 3, width * 3 // 2), jnp.bfloat16),
        compiler_params=pltpu.CompilerParams(vmem_limit_bytes=40 * 1024 * 1024),
        cost_estimate=pl.CostEstimate(
            flops=4 * count * width * units, bytes_accessed=12 * 1024 * 1024, transcendentals=0
        ),
    )(core[None].astype(jnp.int32), acts, down_w, down_w)


def exchange(rows):
    return lax.all_to_all(rows, "expert", split_axis=0, concat_axis=0, tiled=True)


def expert_body(
    core_ref, mine_ref, packed_ref, act_grad_ref, gate_w_ref, up_w_ref, router_ref,
    back_ref, x_ref, gate_out_ref, up_out_ref, act_out_ref, logit_ref,
    total, probs_ref, gate_ref, gate_grad_ref,
):
    f32, bf16 = jnp.float32, jnp.bfloat16
    step = pl.program_id(1)

    @pl.when(step == 0)
    def _():
        unpack_body(packed_ref, x_ref)
        probs = softmax_rows(dot(x_ref[...], router_ref[...]))
        probs_ref[...] = probs
        gate_ref[...] = jnp.sum(probs * mine_ref[...], axis=1, keepdims=True)
        gate_grad_ref[...] = jnp.zeros_like(gate_grad_ref)

    x = x_ref[...]
    gate_w, up_w, gate = gate_w_ref[...], up_w_ref[...], gate_ref[...]
    gate_pre, up_pre = dot(x, gate_w), dot(x, up_w)
    plain = act_grad_ref[...]
    sigmoid = 1.0 / (1.0 + jnp.exp(-gate_pre))
    silu = gate_pre * sigmoid
    act = silu * up_pre
    gate_grad_ref[...] += jnp.sum(act * plain, axis=1, keepdims=True)
    act_grad = gate * plain
    gate_pre_grad = (act_grad * up_pre * sigmoid * (1.0 + gate_pre * (1.0 - sigmoid))).astype(bf16)
    up_pre_grad = (act_grad * silu).astype(bf16)
    gate_out_ref[0] = gate_pre_grad
    up_out_ref[0] = up_pre_grad
    act_out_ref[0] = (gate * act).astype(bf16)
    part = dot_nt(gate_pre_grad, gate_w) + dot_nt(up_pre_grad, up_w)

    @pl.when(step == 0)
    def _():
        total[...] = part

    @pl.when(step > 0)
    def _():
        total[...] += part

    @pl.when(step == pl.num_programs(1) - 1)
    def _():
        logit = (gate_grad_ref[...] * gate * (mine_ref[...] - probs_ref[...])).astype(bf16)
        logit_ref[...] = logit
        pack_block((total[...] + dot_nt(logit, router_ref[...])).astype(bf16), back_ref)


def expert_rows(packed, plain_act_grad, gate_w, up_w, router, core, me):
    f32, bf16 = jnp.float32, jnp.bfloat16
    lines = packed.shape[0]
    width, units = gate_w.shape
    count, experts = lines * 3 // 2, router.shape[1]
    tiles = 4
    block, tile, cut = count // 2, units // tiles, tiles // 2
    mine = (jnp.arange(experts, dtype=jnp.int32) == me).astype(f32)[None, :]
    halves = jax.ShapeDtypeStruct((2, count, units // 2), bf16)
    half_spec = pl.BlockSpec((1, block, tile), lambda i, j, c: ((j // cut + c[0]) % 2, i, j % cut))
    packed_spec = pl.BlockSpec((lines // 2, width * 3 // 2), lambda i, j, c: (i, 0))
    return pl.pallas_call(
        expert_body,
        grid_spec=pltpu.PrefetchScalarGridSpec(
            num_scalar_prefetch=1,
            grid=(2, tiles),
            in_specs=[
                pl.BlockSpec((1, experts), lambda i, j, c: (0, 0)),
                packed_spec,
                pl.BlockSpec((block, tile), lambda i, j, c: (i, j)),
                pl.BlockSpec((width, tile), lambda i, j, c: (0, j)),
                pl.BlockSpec((width, tile), lambda i, j, c: (0, j)),
                pl.BlockSpec((width, experts), lambda i, j, c: (0, 0)),
            ],
            out_specs=[
                packed_spec,
                pl.BlockSpec((block, width), lambda i, j, c: (i, 0)),
                half_spec,
                half_spec,
                half_spec,
                pl.BlockSpec((block, experts), lambda i, j, c: (i, 0)),
            ],
            scratch_shapes=[
                pltpu.VMEM((block, width), f32),
                pltpu.VMEM((block, experts), f32),
                pltpu.VMEM((block, 1), f32),
                pltpu.VMEM((block, 1), f32),
            ],
        ),
        out_shape=[
            jax.ShapeDtypeStruct(packed.shape, bf16),
            jax.ShapeDtypeStruct((count, width), bf16),
            halves,
            halves,
            halves,
            jax.ShapeDtypeStruct((count, experts), bf16),
        ],
        compiler_params=pltpu.CompilerParams(vmem_limit_bytes=48 * 1024 * 1024),
        cost_estimate=pl.CostEstimate(
            flops=8 * count * width * units, bytes_accessed=36 * 1024 * 1024, transcendentals=count * units
        ),
    )(core[None].astype(jnp.int32), mine, packed, plain_act_grad, gate_w, up_w, router)


def output_body(core_ref, heads_ref, weight_ref, inputs_ref, own_ref, other_ref):
    count, half = own_ref.shape
    weight = weight_ref[...].reshape(half, half)
    first = pl.multiple_of(core_ref[0] * count, count)
    second = pl.multiple_of((1 - core_ref[0]) * count, count)
    other_ref[...] = dot(heads_ref[pl.ds(second, count), :], weight).astype(jnp.bfloat16)
    own_ref[...] = dot(heads_ref[pl.ds(first, count), :], weight) + inputs_ref[...].astype(
        jnp.float32
    )


def output_shares(heads, stacked, inputs, core):
    tokens, width = inputs.shape
    half = width // 2
    return pl.pallas_call(
        output_body,
        grid_spec=pltpu.PrefetchScalarGridSpec(
            num_scalar_prefetch=1,
            grid=(2,),
            in_specs=[
                pl.BlockSpec((2 * tokens, half), lambda h, c: (0, 0)),
                pl.BlockSpec((64, half // 64, half), lambda h, c: (0, h, 1)),
                pl.BlockSpec((tokens, half), lambda h, c: (0, h)),
            ],
            out_specs=[pl.BlockSpec((tokens, half), lambda h, c: (0, h))] * 2,
        ),
        out_shape=[
            jax.ShapeDtypeStruct((tokens, width), jnp.float32),
            jax.ShapeDtypeStruct((tokens, width), jnp.bfloat16),
        ],
        compiler_params=pltpu.CompilerParams(vmem_limit_bytes=32 * 1024 * 1024),
    )(core[None].astype(jnp.int32), heads, stacked, inputs)


def heads_body(grad_ref, weight_ref, out_ref, total):
    half = out_ref.shape[1]
    part = dot_nt(grad_ref[...], weight_ref[...].reshape(half, half))

    @pl.when(pl.program_id(0) == 0)
    def _():
        total[...] = part

    @pl.when(pl.program_id(0) == 1)
    def _():
        out_ref[...] = (total[...] + part).astype(jnp.bfloat16)


def heads_grad(grad, stacked):
    tokens, width = grad.shape
    half = width // 2
    return pl.pallas_call(
        heads_body,
        grid=(2,),
        in_specs=[
            pl.BlockSpec((tokens, half), lambda h: (0, h)),
            pl.BlockSpec((64, half // 64, half), lambda h: (0, h, 1)),
        ],
        out_specs=pl.BlockSpec((tokens, half), lambda h: (0, 0)),
        out_shape=jax.ShapeDtypeStruct((tokens, half), jnp.bfloat16),
        scratch_shapes=[pltpu.VMEM((tokens, half), jnp.float32)],
        compiler_params=pltpu.CompilerParams(vmem_limit_bytes=32 * 1024 * 1024),
    )(grad, stacked)


def share_body(core_ref, lows_ref, both_w_ref, value_w_ref, own_ref, other_ref):
    tokens = own_ref.shape[0]
    middle = both_w_ref.shape[1]
    first = pl.ds(pl.multiple_of(core_ref[0] * tokens, tokens), tokens)
    second = pl.ds(pl.multiple_of((1 - core_ref[0]) * tokens, tokens), tokens)
    for rows, out_ref in ((second, other_ref), (first, own_ref)):
        share = dot_nt(lows_ref[rows, :middle], both_w_ref[...]) + dot_nt(
            lows_ref[rows, middle:], value_w_ref[...]
        )
        out_ref[...] = share.astype(out_ref.dtype)


def input_shares(lows, both_w, value_w, core):
    tokens, width = lows.shape[0] // 2, both_w.shape[0]
    half, tile = value_w.shape[1] // 2, width // 8
    return pl.pallas_call(
        share_body,
        grid_spec=pltpu.PrefetchScalarGridSpec(
            num_scalar_prefetch=1,
            grid=(8,),
            in_specs=[
                pl.BlockSpec(lows.shape, lambda i, c: (0, 0)),
                pl.BlockSpec((tile, width), lambda i, c: (i, 0)),
                pl.BlockSpec((tile, half), lambda i, c: (i, 0)),
            ],
            out_specs=[pl.BlockSpec((tokens, tile), lambda i, c: (0, i))] * 2,
        ),
        out_shape=[
            jax.ShapeDtypeStruct((tokens, width), jnp.float32),
            jax.ShapeDtypeStruct((tokens, width), jnp.bfloat16),
        ],
        compiler_params=pltpu.CompilerParams(vmem_limit_bytes=32 * 1024 * 1024),
        cost_estimate=pl.CostEstimate(
            flops=24 * 1000 * 1000 * 1000, bytes_accessed=16 * 1024 * 1024, transcendentals=0
        ),
    )(core[None].astype(jnp.int32), lows, both_w, value_w)


def shards(
    block_entry_states,
    block_result_cotangent,
    token_assignments,
    packed_segment_sizes,
    admitted_route_quota,
    mixing_scale_factor,
    asker_projection,
    lookup_projection,
    content_projection,
    mixing_projection_back,
    asker_scale_factor,
    lookup_scale_factor,
    specialist_scale_factor,
    dispatcher_projection,
    specialist_switch_tensor,
    specialist_widen_tensor,
    specialist_shrink_tensor,
):
    bf16, f32 = jnp.bfloat16, jnp.float32
    tokens_dev = block_entry_states.shape[1]
    width = block_entry_states.shape[2]
    core = lax.axis_index("dp")
    me = lax.axis_index("expert")
    row_len = tokens_dev * 2
    heads_local = HEADS // 2
    head_width = width // HEADS
    half_width = width // 2
    score_scale = head_width ** (-0.5)
    experts = dispatcher_projection.shape[1]

    stacked_output = jnp.concatenate(
        [mixing_projection_back[:, :half_width], mixing_projection_back[:, half_width:]], axis=0
    )
    value_output = lax.all_gather(
        jnp.concatenate([content_projection, stacked_output], axis=1),
        "expert",
        axis=0,
        tiled=True,
    )
    stacked_output = value_output.reshape(64, width // 64, width)
    blocks = jnp.concatenate([asker_projection, lookup_projection], axis=1)
    for step in range(3):
        blocks = jnp.concatenate([blocks, permute_step(blocks, 0, step)], axis=0)
    cuts = (0, 768, 1408, 2048)
    pieces = [[blocks[:, cuts[k] : cuts[k + 1]]] for k in range(3)]
    for k in range(3):
        got = permute_step(pieces[k][0], k, 3)
        pieces[k] = [jnp.concatenate([pieces[k][0], got], axis=0)]
    for k in range(3):
        pieces[k].append(permute_step(pieces[k][0], k, 4))
    for k in range(3):
        pieces[k] += [permute_step(piece, k, 5) for piece in pieces[k]]
    orders = [relative_order(core, me, part) for part in range(3)]
    inverses = [natural_order(order) for order in orders]

    assigned = token_assignments[0]
    expert_iota = jnp.arange(experts, dtype=jnp.int32)
    chosen = jnp.any(assigned[:, :, None] == expert_iota[None, None, :], axis=1)
    token_iota = jnp.arange(tokens_dev, dtype=jnp.int32)
    earlier = (token_iota[:, None] > token_iota[None, :]).astype(bf16)
    rank = dot(earlier, chosen.astype(bf16))
    kept = chosen & (rank < admitted_route_quota.astype(f32)[None, :])
    sent_counts = jnp.sum(kept.astype(jnp.int32), axis=0, dtype=jnp.int32)
    line_iota = jnp.arange(experts * 8, dtype=jnp.int32)
    line = line_iota % 8
    spread = (expert_iota[:, None] == (line_iota // 8)[None, :]).astype(bf16)
    slot_of_line = dot(jnp.where(kept, rank, -1.0).astype(bf16), spread).astype(jnp.int32)
    main = (slot_of_line == line[None, :]).astype(bf16)
    spare_hit = slot_of_line == (8 + line // 2)[None, :]
    spare = jnp.concatenate(
        [spare_hit & (line % 2 == half)[None, :] for half in range(2)], axis=0
    ).astype(bf16)

    lengths = packed_segment_sizes[0]
    row_positions = jnp.arange(row_len, dtype=jnp.int32)
    doc_ids, doc_offset = doc_places(lengths, row_positions)
    allowed = (doc_ids[None, :] == doc_ids[:, None]) & (
        row_positions[None, :] <= row_positions[:, None]
    )
    cos_table, sin_table = rope_tables(doc_offset, head_width)
    head_shape = (row_len, heads_local, head_width)
    column_start = core * half_width
    query_half_gain = lax.dynamic_slice_in_dim(asker_scale_factor, column_start, half_width)
    key_half_gain = lax.dynamic_slice_in_dim(lookup_scale_factor, column_start, half_width)

    def whole_row(own):
        other = swap(own)
        return jnp.concatenate(
            [jnp.where(core == 0, own, other), jnp.where(core == 0, other, own)], axis=0
        )

    inputs = block_entry_states[0].astype(f32)
    factor_in = rms_factor(inputs)
    normed_in = (inputs * factor_in * mixing_scale_factor).astype(bf16)
    normed_t = whole_row(normed_in).T
    normed_rel = [reorder(normed_t, order) for order in orders]

    def project(left, pieces):
        size = width // len(pieces)
        return sum(dot_tn(left[i * size : (i + 1) * size], p) for i, p in enumerate(pieces))

    both_proj = jnp.concatenate([project(normed_rel[k], pieces[k]) for k in range(3)], axis=1)
    query_proj, key_proj = both_proj[:, :half_width], both_proj[:, half_width:]
    value_low = dot_tn(normed_t, value_output[:, :half_width]).astype(bf16).reshape(head_shape)
    grad_top_low = block_result_cotangent[0]
    send_grads, *_ = lax.optimization_barrier(
        (to_experts(main, spare, grad_top_low), *(pieces[k][-1] for k in range(3)))
    )
    arrived_grads = exchange(send_grads)
    query_sq, key_sq = lax.psum(
        (jnp.sum(query_proj * query_proj, axis=1), jnp.sum(key_proj * key_proj, axis=1)), "dp"
    )
    query_factor = lax.rsqrt(query_sq[:, None] / width + EPS)
    key_factor = lax.rsqrt(key_sq[:, None] / width + EPS)
    queries = rotate(
        (query_proj * query_factor * query_half_gain).reshape(head_shape), cos_table, sin_table
    ).astype(bf16)
    keys = rotate(
        (key_proj * key_factor * key_half_gain).reshape(head_shape), cos_table, sin_table
    ).astype(bf16)
    raw_scores = jnp.einsum("qhd,khd->hqk", queries, keys, preferred_element_type=f32) * score_scale
    attn_probs = softmax_rows(jnp.where(allowed[None], raw_scores, NEG))
    attn_low = attn_probs.astype(bf16)
    mixed_heads = (
        jnp.einsum("hqk,khd->qhd", attn_low, value_low, preferred_element_type=f32)
        .reshape(row_len, half_width)
        .astype(bf16)
    )
    hidden_own, share_other = output_shares(
        mixed_heads, stacked_output, block_entry_states[0], core
    )
    hidden = hidden_own + swap(share_other).astype(f32)
    factor_moe = rms_factor(hidden)
    normed_moe = (hidden * factor_moe * specialist_scale_factor).astype(bf16)

    arrived = exchange(to_experts(main, spare, normed_moe))
    *late_pieces, _ = lax.optimization_barrier((*pieces, normed_moe))
    both_w = jnp.concatenate(
        [reorder(jnp.concatenate(late_pieces[k], axis=0), inverses[k]) for k in range(3)], axis=1
    )
    both_w, arrived = lax.optimization_barrier((both_w, arrived))
    gate_w, up_w, down_w = (
        specialist_switch_tensor[0],
        specialist_widen_tensor[0],
        specialist_shrink_tensor[0],
    )
    top_rows = unpack(arrived_grads)
    plain_act_grad = dot_nt(top_rows, down_w)
    row_grad, rows_in, gate_pre_grad, up_pre_grad, gated_act, logit_grad = expert_rows(
        arrived, plain_act_grad, gate_w, up_w, dispatcher_projection, core, me
    )
    returned_grads = exchange(row_grad)
    send_out, returned_grads = lax.optimization_barrier(
        (expert_results(gated_act, down_w, core), returned_grads)
    )
    returned = exchange(send_out)

    def summed(left, right):
        return left + swap(right.astype(bf16)).astype(f32)

    gate_weight_grad = summed(dot_tn(rows_in, gate_pre_grad[0]), dot_tn(rows_in, gate_pre_grad[1]))
    up_weight_grad = summed(dot_tn(rows_in, up_pre_grad[0]), dot_tn(rows_in, up_pre_grad[1]))
    down_weight_grad = summed(dot_tn(gated_act[0], top_rows), dot_tn(gated_act[1], top_rows))

    moe_in_grad = from_experts(main, spare, returned_grads)
    hidden_norm_grad, moe_gain_local = norm_back(
        moe_in_grad, hidden, factor_moe, specialist_scale_factor
    )
    hidden_grad = grad_top_low.astype(f32) + hidden_norm_grad
    grad_full = whole_row(hidden_grad.astype(bf16))
    mixed_grad = heads_grad(grad_full, stacked_output).reshape(head_shape)
    mixed_rel = reorder(mixed_heads.T, orders[0])
    output_rows, output_got = width // 128, []
    for step in reversed(range(STEPS)):
        low, high = 1 << step, 2 << step
        piece = dot(mixed_rel[low * output_rows : high * output_rows], grad_full)
        for g in output_got:
            piece = piece + g[low * output_rows : high * output_rows].astype(f32)
        output_got.append(permute_step(piece.astype(bf16), 0, step))
    output_weight_grad = dot(mixed_rel[:output_rows], grad_full)
    for g in output_got:
        output_weight_grad = output_weight_grad + g[:output_rows].astype(f32)
    prob_grad_att = jnp.einsum("qhd,khd->hqk", mixed_grad, value_low, preferred_element_type=f32)
    score_grad = (
        attn_probs * (prob_grad_att - jnp.sum(attn_probs * prob_grad_att, axis=-1, keepdims=True))
    ).astype(bf16)
    value_grad = jnp.einsum("hqk,qhd->khd", attn_low, mixed_grad, preferred_element_type=f32)
    query_rot_grad = (
        jnp.einsum("hqk,khd->qhd", score_grad, keys, preferred_element_type=f32) * score_scale
    )
    key_rot_grad = (
        jnp.einsum("hqk,qhd->khd", score_grad, queries, preferred_element_type=f32) * score_scale
    )
    query_norm_grad = unrotate(query_rot_grad, cos_table, sin_table).reshape(row_len, half_width)
    key_norm_grad = unrotate(key_rot_grad, cos_table, sin_table).reshape(row_len, half_width)
    query_scaled = query_norm_grad * query_half_gain
    key_scaled = key_norm_grad * key_half_gain
    query_inner, key_inner = lax.psum(
        (jnp.sum(query_scaled * query_proj, axis=1), jnp.sum(key_scaled * key_proj, axis=1)), "dp"
    )
    query_low = (
        query_factor
        * (query_scaled - query_proj * query_factor * query_factor * (query_inner[:, None] / width))
    ).astype(bf16)
    key_low = (
        key_factor
        * (key_scaled - key_proj * key_factor * key_factor * (key_inner[:, None] / width))
    ).astype(bf16)
    value_proj_low = value_grad.reshape(row_len, half_width).astype(bf16)
    empty_gain = jnp.zeros((width,), f32)
    query_gain_local = lax.dynamic_update_slice_in_dim(
        empty_gain, jnp.sum(query_norm_grad * query_proj * query_factor, axis=0), column_start, 0
    )
    key_gain_local = lax.dynamic_update_slice_in_dim(
        empty_gain, jnp.sum(key_norm_grad * key_proj * key_factor, axis=0), column_start, 0
    )
    lows = (query_low, key_low, value_proj_low)

    def left_of(k, low, high):
        return normed_rel[k][low * (width // 64) : high * (width // 64)]

    sent = [dot(left_of(k, 32, 64), lows[k]).astype(bf16) for k in range(3)]
    *sent, share_lows, returned = lax.optimization_barrier((*sent, lows, returned))
    share_own, share_other = input_shares(
        jnp.concatenate(share_lows, axis=1), both_w, value_output, core
    )
    got = [[permute_step(sent[k], k, 5)] for k in range(3)]
    rows = width // 64
    for step in (4, 3):
        low, high = 1 << step, 2 << step
        for k in range(3):
            piece = dot(left_of(k, low, high), lows[k])
            for g in got[k]:
                piece = piece + g[low * rows : high * rows].astype(f32)
            got[k].append(permute_step(piece.astype(bf16), k, step))
    near = [sum(g[: 8 * rows].astype(f32) for g in got[k]) for k in range(3)]
    projection_grads, output_weight_grad = lax.optimization_barrier(
        (jnp.concatenate(near, axis=1), output_weight_grad)
    )
    low_all = jnp.concatenate(lows, axis=1)
    for step in (2, 1, 0):
        low, high = 1 << step, 2 << step
        piece = dot(left_of(0, low, high), low_all) + projection_grads[low * rows :]
        projection_grads = projection_grads[: low * rows] + permute_step(
            piece.astype(bf16), 0, step
        ).astype(f32)
    projection_grads = projection_grads + dot(left_of(0, 0, 1), low_all)
    block_output = hidden + from_experts(main, spare, returned)
    normed_in_grad = share_own + swap(share_other).astype(f32)
    input_norm_grad, attn_gain_local = norm_back(
        normed_in_grad, inputs, factor_in, mixing_scale_factor
    )
    input_grad = hidden_grad + input_norm_grad

    own_counts = jnp.where(
        (jnp.arange(2)[:, None, None] == core) & (expert_iota[None, :, None] == me),
        sent_counts[None, None, :],
        0,
    ).astype(f32)
    totals = sum_everywhere(
        jnp.concatenate(
            [
                dot_tn(logit_grad, rows_in),
                own_counts.reshape(2 * experts * experts // width, width),
                jnp.stack([attn_gain_local, query_gain_local, key_gain_local, moe_gain_local]),
            ]
        ),
        core,
        1,
    )
    router_weight_grad, all_counts, gains = totals[:experts].T, totals[experts:-4], totals[-4:]
    got_counts = jnp.sum(
        jnp.where(
            (jnp.arange(2)[:, None, None] == core) & (expert_iota[None, None, :] == me),
            all_counts.reshape(2, experts, experts),
            0.0,
        ),
        axis=(0, 2),
    ).astype(jnp.int32)
    return (
        block_output[None],
        input_grad[None],
        gains[0],
        projection_grads[:, :half_width],
        projection_grads[:, half_width : 2 * half_width],
        projection_grads[:, 2 * half_width :],
        output_weight_grad,
        gains[1],
        gains[2],
        gains[3],
        router_weight_grad,
        gate_weight_grad[None],
        up_weight_grad[None],
        down_weight_grad[None],
        got_counts[None],
    )


def solution(mesh):
    placed = (
        P("expert", "dp", None),
        P("expert", "dp", None),
        P("expert", "dp", None),
        P("expert", None),
        P(),
        P(),
        P("expert", "dp"),
        P("expert", "dp"),
        P("expert", "dp"),
        P(("dp", "expert"), None),
        P(),
        P(),
        P(),
        P(),
        P("expert", None, None),
        P("expert", None, None),
        P("expert", None, None),
    )
    return jax.shard_map(
        shards,
        mesh=mesh,
        in_specs=placed,
        out_specs=(
            P("expert", "dp", None),
            P("expert", "dp", None),
            P(),
            P("expert", "dp"),
            P("expert", "dp"),
            P("expert", "dp"),
            P(("dp", "expert"), None),
            P(),
            P(),
            P(),
            P(),
            P("expert", None, "dp"),
            P("expert", None, "dp"),
            P("expert", "dp", None),
            P("expert", "dp"),
        ),
        check_vma=False,
    )
```

time: 1220 us -> 555 us (0.45)
  waiting for transfers between devices: 764 us -> 152 us
  local copies, waits for them, and re-layouts: 150 us -> 70 us
  Pallas kernels: 0 us -> 57 us
  starting transfers between devices: 38.2 us -> 91.9 us
  other arithmetic: 107 us -> 67.8 us
  matrix products: 112 us -> 84.3 us
  blocking collectives: 25.5 us -> 5.6 us
    unnamed x10 -> x1, waiting for transfers between devices: 417 us -> 0.02 us
    all_gather x4 -> x1, waiting for transfers between devices: 156 us -> 0.01 us  [shards(): lax.all_gather(jnp.concatenate([content_projection, stacked_output], axis...]
    ppermute x0 -> x48, waiting for transfers between devices: none -> 110 us  [the longest x39 110 us: permute_step(): return lax.ppermute(value, BOTH, pairs)]
    all_to_all x5 -> x4, waiting for transfers between devices: 134 us -> 41.4 us  [exchange(): lax.all_to_all(rows, 'expert', split_axis=0, concat_axis=0, tiled=True)]
    ppermute x0 -> x48, starting transfers between devices: none -> 59.6 us  [the longest x39 57.5 us: permute_step(): return lax.ppermute(value, BOTH, pairs)]
    pallas_call x0 -> x10, Pallas kernels: none -> 57 us  [the longest x1 27.1 us: expert_rows(): pl.pallas_call(expert_body, grid_spec=pltpu.PrefetchScalarGridSpec(num_sc...]
    psum x1 -> x0, waiting for transfers between devices: 35.4 us -> none  [in_one(): so_far = lax.psum(ravelled, axis)]
    reshape x9 -> x2, local copies, waits for them, and re-layouts: 35.6 us -> 2.11 us  [the longest x1 2.01 us: shards(): mixed_grad = heads_grad(grad_full, stacked_output).reshape(head_shape)]
  transfers between devices with their start and end apart: 14 -> 53, of which waited for: 12 -> 23; matrix products, arithmetic and copies ran while one was open for 22% -> 33% of each run, Pallas kernels for 0% -> 5%
where the time goes in v1:
time: 555 us; the launch traced here: 545 us
  waiting for transfers between devices  152 us (27%)
  starting transfers between devices  91.9 us (17%)
  matrix products  84.3 us (15%)
  local copies, waits for them, and re-layouts  70 us (13%)
  other arithmetic  67.8 us (12%)
  Pallas kernels  57 us (10%)
  between operations  16.8 us (3%)
  blocking collectives  5.6 us (1%)
    ppermute x39, waiting for transfers between devices, permute_step(): return lax.ppermute(value, BOTH, pairs)  110 us
    ppermute x39, starting transfers between devices, permute_step(): return lax.ppermute(value, BOTH, pairs)  57.5 us
    dot_general x20, matrix products, dot_tn(): lax.dot_general(left, right, (((0,), (0,)), ((), ())), preferred_element_...  45.5 us
    all_to_all x4, waiting for transfers between devices, exchange(): lax.all_to_all(rows, 'expert', split_axis=0, concat_axis=0, tiled=True)  41.4 us
    unnamed x310, local copies, waits for them, and re-layouts  35.7 us
    all_to_all x4, starting transfers between devices, exchange(): lax.all_to_all(rows, 'expert', split_axis=0, concat_axis=0, tiled=True)  32.3 us
    pallas_call x1, Pallas kernels, expert_rows(): pl.pallas_call(expert_body, grid_spec=pltpu.PrefetchScalarGridSpec(num_sc...  27.1 us
    dot_general x22, matrix products, dot(): return jnp.dot(left, right, preferred_element_type=jnp.float32)  25 us
  transfers between devices with their start and end apart: 53, of which 23 were waited for; matrix products, arithmetic and copies ran while one was open for 33% of the time, Pallas kernels for 5%

profile of v1, /device:TPU:0, one launch (start us, length us, event | category | flops | bytes accessed | tf_op | source)
XLA Modules:
  0.0 545.1 jit_solution(5534713055916754251)
XLA Ops:
  30.3 5.5 collective-permute-done.3
  72.2 10.6 %collective-permute-done.13 = bf16[512,640]{1,0:T(8,128)(2,1)} collective-permute-done((bf16[512,640]{1,0:T(8,128)(2,1)}, bf16[512,640]{1,0:T(8,128)(2,1)}, u32[]{:S(2)}, u32[]{:S(2)}) %collective-permute-start.13) | collective-permute-done | bytes 655392 | tf_op jit(solution)/shard_map/ppermute | solution.py:35
  89.4 14.4 %collective-permute-done.5 = bf16[512,768]{1,0:T(8,128)(2,1)S(1)} collective-permute-done((bf16[512,768]{1,0:T(8,128)(2,1)S(1)}, bf16[512,768]{1,0:T(8,128)(2,1)S(1)}, u32[]{:S(2)}, u32[]{:S(2)}) %collective-permute-start.5) | collective-permute-done | bytes 786464 | tf_op jit(solution)/shard_map/ppermute | solution.py:35
  111.3 5.8 %collective-permute-done.7 = bf16[512,768]{1,0:T(8,128)(2,1)S(1)} collective-permute-done((bf16[512,768]{1,0:T(8,128)(2,1)S(1)}, bf16[512,768]{1,0:T(8,128)(2,1)S(1)}, u32[]{:S(2)}, u32[]{:S(2)}) %collective-permute-start.7) | collective-permute-done | bytes 786464 | tf_op jit(solution)/shard_map/ppermute | solution.py:35
  122.1 6.8 %all-to-all-start.1 = ((bf16[64,8,3072]{2,1,0:T(8,128)(2,1)}), bf16[64,8,3072]{2,1,0:T(8,128)(2,1)}, u32[]{:S(2)}, u32[]{:S(2)}) async-start(bf16[64,8,3072]{2,1,0:T(8,128)(2,1)} %bitcast.253), calls=%async_computation.1 | async-start | bytes 6291456 | tf_op jit(solution)/shard_map/all_to_all | solution.py:253
  152.4 18.4 %all-to-all-done.1 = bf16[64,8,3072]{2,1,0:T(8,128)(2,1)} async-done(((bf16[64,8,3072]{2,1,0:T(8,128)(2,1)}), bf16[64,8,3072]{2,1,0:T(8,128)(2,1)}, u32[]{:S(2)}, u32[]{:S(2)}) %all-to-all-start.1) | async-done | bytes 3145760 | tf_op jit(solution)/shard_map/all_to_all | solution.py:253
  170.8 7.2 %all-to-all-start = ((bf16[64,8,3072]{2,1,0:T(8,128)(2,1)}), bf16[64,8,3072]{2,1,0:T(8,128)(2,1)}, u32[]{:S(2)}, u32[]{:S(2)}) async-start(bf16[64,8,3072]{2,1,0:T(8,128)(2,1)} %bitcast.31), calls=%async_computation | async-start | bytes 6291456 | tf_op jit(solution)/shard_map/all_to_all | solution.py:253
  212.4 7.2 %pad_maximum_fusion.both_w_ref = bf16[2048,2048]{1,0:T(8,128)(2,1)} fusion(bf16[2048,640]{1,0:T(8,128)(2,1)} %bitcast.263, bf16[2048,640]{1,0:T(8,128)(2,1)} %bitcast.264, bf16[2048,768]{1,0:T(8,128)(2,1)} %bitcast.259), kind=kLoop, calls=%fused_computation.8 | loop fusion | flops 25165824 | bytes 16777216 | tf_op jit(solution)/shard_map/concatenate | solution.py:597
  220.6 27.1 %shard_map.338 = (bf16[512,3072]{1,0:T(8,128)(2,1)}, bf16[768,2048]{1,0:T(8,128)(2,1)}, bf16[2,768,512]{2,1,0:T(8,128)(2,1)S(1)}, bf16[2,768,512]{2,1,0:T(8,128)...) custom-call(s32[1]{0:T(128)} %bitcast.core_ref, f32[1,64]{1,0:T(1,128)S(1)} %compare_convert_fusion.1.mine_ref, ...), custom_call_target="tpu_custom_call" | custom-call | flops 12884901888 | bytes 37748736 | tf_op jit(solution)/shard_map/pallas_call | solution.py:314
  251.8 10.7 %all-to-all-start.2 = ((bf16[64,8,3072]{2,1,0:T(8,128)(2,1)}), bf16[64,8,3072]{2,1,0:T(8,128)(2,1)}, u32[]{:S(2)}, u32[]{:S(2)}) async-start(bf16[64,8,3072]{2,1,0:T(8,128)(2,1)} %bitcast.279), calls=%async_computation.2 | async-start | bytes 6291456 | tf_op jit(solution)/shard_map/all_to_all | solution.py:253
  268.0 5.4 convolution_convert_fusion.3
  280.1 23.0 %all-to-all-done.2 = bf16[64,8,3072]{2,1,0:T(8,128)(2,1)} async-done(((bf16[64,8,3072]{2,1,0:T(8,128)(2,1)}), bf16[64,8,3072]{2,1,0:T(8,128)(2,1)}, u32[]{:S(2)}, u32[]{:S(2)}) %all-to-all-start.2) | async-done | bytes 3145760 | tf_op jit(solution)/shard_map/all_to_all | solution.py:253
  315.8 7.6 %all-to-all-start.3 = ((bf16[64,8,3072]{2,1,0:T(8,128)(2,1)}), bf16[64,8,3072]{2,1,0:T(8,128)(2,1)}, u32[]{:S(2)}, u32[]{:S(2)}) async-start(bf16[64,8,3072]{2,1,0:T(8,128)(2,1)} %bitcast.254), calls=%async_computation.3 | async-start | bytes 6291456 | tf_op jit(solution)/shard_map/all_to_all | solution.py:253
  370.0 16.2 %collective-permute-done.36 = bf16[512,2048]{1,0:T(8,128)(2,1)} collective-permute-done((bf16[512,2048]{1,0:T(8,128)(2,1)}, bf16[512,2048]{1,0:T(8,128)(2,1)}, u32[]{:S(2)}, u32[]{:S(2)}) %collective-permute-start.36) | collective-permute-done | bytes 2097184 | tf_op jit(solution)/shard_map/ppermute | solution.py:35
  398.7 9.7 %shard_map.343 = (f32[128,2048]{1,0:T(8,128)S(1)}, bf16[128,2048]{1,0:T(8,128)(2,1)S(1)}) custom-call(s32[1]{0:T(128)} %bitcast.core_ref, bf16[256,3072]{1,0:T(8,128)(2,1)S(1)} %pad_maximum_fusion.5.lows_ref, bf16[2048,2048]{1,0:T(8,128)(2,1)S(1)} %copy-done.12, bf16[2048,2048]{1,0:T(8,128)(2,1)S(1)} %copy-done.2), custom_call_target="tpu_custom_call" | custom-call | flops 24000000000 | bytes 16777216 | tf_op jit(solution)/shard_map/pallas_call | solution.py:436
  422.6 5.7 %add_bitcast_fusion.2 = f32[1,2048,512]{2,1,0:T(8,128)} fusion(bf16[2048,512]{1,0:T(8,128)(2,1)} %collective-permute-done.45, bf16[768,2048]{1,0:T(8,128)(2,1)S(1)} %copy-done.65, bf16[2,768,512]{2,1,0:T(8,128)(2,1)S(1)} %copy-done.30), kind=kOutput, calls=%fused_computation.13 | convolution fusion | flops 1612709888 | bytes 10223616 | tf_op jit(solution)/shard_map/dot_general | solution.py:73
  435.3 5.5 %add_bitcast_fusion.1 = f32[1,2048,512]{2,1,0:T(8,128)} fusion(bf16[2048,512]{1,0:T(8,128)(2,1)} %collective-permute-done.46, bf16[768,2048]{1,0:T(8,128)(2,1)S(1)} %copy-done.65, bf16[2,768,512]{2,1,0:T(8,128)(2,1)S(1)} %copy-done.28), kind=kOutput, calls=%fused_computation.12 | convolution fusion | flops 1612709888 | bytes 10223616 | tf_op jit(solution)/shard_map/dot_general | solution.py:73
  446.7 5.4 add_bitcast_fusion
  452.1 7.9 %collective-permute-done.22 = f32[72,1024]{1,0:T(8,128)S(1)} collective-permute-done((f32[72,1024]{1,0:T(8,128)S(1)}, f32[72,1024]{1,0:T(8,128)S(1)}, u32[]{:S(2)}, u32[]{:S(2)}) %collective-permute-start.22) | collective-permute-done | bytes 294944 | tf_op jit(solution)/shard_map/ppermute | solution.py:35
  484.7 6.9 %collective-permute-done.25 = f32[72,1024]{1,0:T(8,128)S(1)} collective-permute-done((f32[72,1024]{1,0:T(8,128)S(1)}, f32[72,1024]{1,0:T(8,128)S(1)}, u32[]{:S(2)}, u32[]{:S(2)}) %collective-permute-start.25) | collective-permute-done | bytes 294944 | tf_op jit(solution)/shard_map/ppermute | solution.py:35
  496.8 5.8 %collective-permute-done.35 = bf16[256,1024]{1,0:T(8,128)(2,1)S(1)} collective-permute-done((bf16[256,1024]{1,0:T(8,128)(2,1)S(1)}, bf16[256,1024]{1,0:T(8,128)(2,1)S(1)}, u32[]{:S(2)}, u32[]{:S(2)}) %collective-permute-start.35) | collective-permute-done | bytes 524320 | tf_op jit(solution)/shard_map/ppermute | solution.py:35
  512.3 7.6 %collective-permute-done.42 = bf16[128,3072]{1,0:T(8,128)(2,1)S(1)} collective-permute-done((bf16[128,3072]{1,0:T(8,128)(2,1)S(1)}, bf16[128,3072]{1,0:T(8,128)(2,1)S(1)}, u32[]{:S(2)}, u32[]{:S(2)}) %collective-permute-start.42) | collective-permute-done | bytes 786464 | tf_op jit(solution)/shard_map/ppermute | solution.py:35
  522.5 7.0 %collective-permute-done.43 = bf16[64,3072]{1,0:T(8,128)(2,1)} collective-permute-done((bf16[64,3072]{1,0:T(8,128)(2,1)}, bf16[64,3072]{1,0:T(8,128)(2,1)}, u32[]{:S(2)}, u32[]{:S(2)}) %collective-permute-start.43) | collective-permute-done | bytes 393248 | tf_op jit(solution)/shard_map/ppermute | solution.py:35
  531.9 5.1 collective-permute-done.44
  (599 shorter events, 295.8 us)
Async XLA Ops:
  7.3 128.2 %all-gather.2.cloned.1.call-start = ((), (), s32[]{:S(2)}) async-start(), calls=%async_computation.4 | async-start | bytes 8519680 | tf_op jit(solution)/shard_map/all_gather | solution.py:493
  57.1 25.7 %collective-permute-start.13 = (bf16[512,640]{1,0:T(8,128)(2,1)}, bf16[512,640]{1,0:T(8,128)(2,1)}, u32[]{:S(2)}, u32[]{:S(2)}) collective-permute-start(bf16[512,640]{1,0:T(8,128)(2,1)} %pad_maximum_fusion.15), channel_id=1, source_target_pairs={{0,3},{1,2},{2,1},{3,0},{4,7},{5,6},{6,5},{7,4},{8,11},{9,10},{10,... | collective-permute-start | bytes 1966088 | tf_op jit(solution)/shard_map/ppermute | solution.py:35
  60.7 26.7 %collective-permute-start.14 = (bf16[512,640]{1,0:T(8,128)(2,1)}, bf16[512,640]{1,0:T(8,128)(2,1)S(1)}, u32[]{:S(2)}, u32[]{:S(2)}) collective-permute-start(bf16[512,640]{1,0:T(8,128)(2,1)} %pad_maximum_fusion.15), channel_id=1, source_target_pairs={{0,12},{1,13},{2,14},{3,15},{4,8},{5,9},{6,10},{7,11},{8,4},{9,5},... | collective-permute-start | bytes 1966088 | tf_op jit(solution)/shard_map/ppermute | solution.py:35
  65.6 38.7 %collective-permute-start.6 = (bf16[512,768]{1,0:T(8,128)(2,1)S(1)}, bf16[512,768]{1,0:T(8,128)(2,1)S(1)}, u32[]{:S(2)}, u32[]{:S(2)}) collective-permute-start(bf16[512,768]{1,0:T(8,128)(2,1)S(1)} %pad_maximum_fusion.12), channel_id=1, source_target_pairs={{0,48},{1,49},{2,50},{3,51},{4,52},{5,53},{6,54},{7,55},{8,56},{9,... | collective-permute-start | bytes 2359304 | tf_op jit(solution)/shard_map/ppermute | solution.py:35
  66.4 37.4 %collective-permute-start.5 = (bf16[512,768]{1,0:T(8,128)(2,1)S(1)}, bf16[512,768]{1,0:T(8,128)(2,1)S(1)}, u32[]{:S(2)}, u32[]{:S(2)}) collective-permute-start(bf16[512,768]{1,0:T(8,128)(2,1)S(1)} %pad_maximum_fusion.12), channel_id=1, source_target_pairs={{0,12},{1,13},{2,14},{3,15},{4,8},{5,9},{6,10},{7,11},{8,4},{9,5},... | collective-permute-start | bytes 2359304 | tf_op jit(solution)/shard_map/ppermute | solution.py:35
  69.8 36.4 %collective-permute-start.11 = (bf16[512,640]{1,0:T(8,128)(2,1)}, bf16[512,640]{1,0:T(8,128)(2,1)S(1)}, u32[]{:S(2)}, u32[]{:S(2)}) collective-permute-start(bf16[512,640]{1,0:T(8,128)(2,1)} %collective-permute-done.9), channel_id=1, source_target_pairs={{0,3},{1,2},{2,1},{3,0},{4,7},{5,6},{6,5},{7,4},{8,11},{9,10},{10,... | collective-permute-start | bytes 1966088 | tf_op jit(solution)/shard_map/ppermute | solution.py:35
  82.9 28.0 %collective-permute-start.15 = (bf16[512,640]{1,0:T(8,128)(2,1)}, bf16[512,640]{1,0:T(8,128)(2,1)S(1)}, u32[]{:S(2)}, u32[]{:S(2)}) collective-permute-start(bf16[512,640]{1,0:T(8,128)(2,1)} %collective-permute-done.13), channel_id=1, source_target_pairs={{0,12},{1,13},{2,14},{3,15},{4,8},{5,9},{6,10},{7,11},{8,4},{9,5},... | collective-permute-start | bytes 1966088 | tf_op jit(solution)/shard_map/ppermute | solution.py:35
  122.1 48.7 %all-to-all-start.1 = ((bf16[64,8,3072]{2,1,0:T(8,128)(2,1)}), bf16[64,8,3072]{2,1,0:T(8,128)(2,1)}, u32[]{:S(2)}, u32[]{:S(2)}) async-start(bf16[64,8,3072]{2,1,0:T(8,128)(2,1)} %bitcast.253), calls=%async_computation.1 | async-start | bytes 6291456 | tf_op jit(solution)/shard_map/all_to_all | solution.py:253
  170.8 48.8 %all-to-all-start = ((bf16[64,8,3072]{2,1,0:T(8,128)(2,1)}), bf16[64,8,3072]{2,1,0:T(8,128)(2,1)}, u32[]{:S(2)}, u32[]{:S(2)}) async-start(bf16[64,8,3072]{2,1,0:T(8,128)(2,1)} %bitcast.31), calls=%async_computation | async-start | bytes 6291456 | tf_op jit(solution)/shard_map/all_to_all | solution.py:253
  251.8 51.2 %all-to-all-start.2 = ((bf16[64,8,3072]{2,1,0:T(8,128)(2,1)}), bf16[64,8,3072]{2,1,0:T(8,128)(2,1)}, u32[]{:S(2)}, u32[]{:S(2)}) async-start(bf16[64,8,3072]{2,1,0:T(8,128)(2,1)} %bitcast.279), calls=%async_computation.2 | async-start | bytes 6291456 | tf_op jit(solution)/shard_map/all_to_all | solution.py:253
  273.5 148.8 %collective-permute-start.45 = (bf16[2048,512]{1,0:T(8,128)(2,1)}, bf16[2048,512]{1,0:T(8,128)(2,1)}, u32[]{:S(2)}, u32[]{:S(2)}) collective-permute-start(bf16[2048,512]{1,0:T(8,128)(2,1)} %convolution_convert_fusion.3), channel_id=1, source_target_pairs={{0,64},{64,0},{1,65},{65,1},{2,66},{66,2},{3,67},{67,3},{4,68},{68... | collective-permute-start | bytes 6291464 | tf_op jit(solution)/shard_map/ppermute | solution.py:65
  312.2 121.5 %collective-permute-start.46 = (bf16[2048,512]{1,0:T(8,128)(2,1)}, bf16[2048,512]{1,0:T(8,128)(2,1)}, u32[]{:S(2)}, u32[]{:S(2)}) collective-permute-start(bf16[2048,512]{1,0:T(8,128)(2,1)} %convolution_convert_fusion.2), channel_id=1, source_target_pairs={{0,64},{64,0},{1,65},{65,1},{2,66},{66,2},{3,67},{67,3},{4,68},{68... | collective-permute-start | bytes 6291464 | tf_op jit(solution)/shard_map/ppermute | solution.py:65
  315.3 129.3 %collective-permute-start.47 = (bf16[512,2048]{1,0:T(8,128)(2,1)}, bf16[512,2048]{1,0:T(8,128)(2,1)}, u32[]{:S(2)}, u32[]{:S(2)}) collective-permute-start(bf16[512,2048]{1,0:T(8,128)(2,1)} %convolution_convert_fusion.1), channel_id=1, source_target_pairs={{0,64},{64,0},{1,65},{65,1},{2,66},{66,2},{3,67},{67,3},{4,68},{68... | collective-permute-start | bytes 6291464 | tf_op jit(solution)/shard_map/ppermute | solution.py:65
  315.8 74.6 %all-to-all-start.3 = ((bf16[64,8,3072]{2,1,0:T(8,128)(2,1)}), bf16[64,8,3072]{2,1,0:T(8,128)(2,1)}, u32[]{:S(2)}, u32[]{:S(2)}) async-start(bf16[64,8,3072]{2,1,0:T(8,128)(2,1)} %bitcast.254), calls=%async_computation.3 | async-start | bytes 6291456 | tf_op jit(solution)/shard_map/all_to_all | solution.py:253
  341.8 44.4 %collective-permute-start.36 = (bf16[512,2048]{1,0:T(8,128)(2,1)}, bf16[512,2048]{1,0:T(8,128)(2,1)}, u32[]{:S(2)}, u32[]{:S(2)}) collective-permute-start(bf16[512,2048]{1,0:T(8,128)(2,1)} %convolution_convert_fusion), channel_id=1, source_target_pairs={{0,48},{1,49},{2,50},{3,51},{4,52},{5,53},{6,54},{7,55},{8,56},{9,... | collective-permute-start | bytes 6291464 | tf_op jit(solution)/shard_map/ppermute | solution.py:35
  388.9 28.9 %collective-permute-start.37 = (bf16[256,2048]{1,0:T(8,128)(2,1)}, bf16[256,2048]{1,0:T(8,128)(2,1)}, u32[]{:S(2)}, u32[]{:S(2)}) collective-permute-start(bf16[256,2048]{1,0:T(8,128)(2,1)} %fusion.4), channel_id=1, source_target_pairs={{0,12},{1,13},{2,14},{3,15},{4,8},{5,9},{6,10},{7,11},{8,4},{9,5},... | collective-permute-start | bytes 3145736 | tf_op jit(solution)/shard_map/ppermute | solution.py:35
  417.8 53.8 %collective-permute-start.33 = (bf16[1024,1024]{1,0:T(8,128)(2,1)}, bf16[1024,1024]{1,0:T(8,128)(2,1)S(1)}, u32[]{:S(2)}, u32[]{:S(2)}) collective-permute-start(bf16[1024,1024]{1,0:T(8,128)(2,1)} %convolution_convert_fusion.4), channel_id=1, source_target_pairs={{0,12},{1,13},{2,14},{3,15},{4,8},{5,9},{6,10},{7,11},{8,4},{9,5},... | collective-permute-start | bytes 6291464 | tf_op jit(solution)/shard_map/ppermute | solution.py:35
  431.3 41.9 %collective-permute-start.30 = (bf16[1024,1024]{1,0:T(8,128)(2,1)S(1)}, bf16[1024,1024]{1,0:T(8,128)(2,1)S(1)}, u32[]{:S(2)}, u32[]{:S(2)}) collective-permute-start(bf16[1024,1024]{1,0:T(8,128)(2,1)S(1)} %copy-done.79), channel_id=1, source_target_pairs={{0,3},{1,2},{2,1},{3,0},{4,7},{5,6},{6,5},{7,4},{8,11},{9,10},{10,... | collective-permute-start | bytes 6291464 | tf_op jit(solution)/shard_map/ppermute | solution.py:35
  433.6 41.4 %collective-permute-start.27 = (bf16[1024,1024]{1,0:T(8,128)(2,1)S(1)}, bf16[1024,1024]{1,0:T(8,128)(2,1)S(1)}, u32[]{:S(2)}, u32[]{:S(2)}) collective-permute-start(bf16[1024,1024]{1,0:T(8,128)(2,1)S(1)} %copy-done.78), channel_id=1, source_target_pairs={{0,48},{1,49},{2,50},{3,51},{4,52},{5,53},{6,54},{7,55},{8,56},{9,... | collective-permute-start | bytes 6291464 | tf_op jit(solution)/shard_map/ppermute | solution.py:35
  444.5 21.1 %collective-permute-start.39 = (bf16[64,2048]{1,0:T(8,128)(2,1)S(1)}, bf16[64,2048]{1,0:T(8,128)(2,1)S(1)}, u32[]{:S(2)}, u32[]{:S(2)}) collective-permute-start(bf16[64,2048]{1,0:T(8,128)(2,1)S(1)} %fusion.9), channel_id=1, source_target_pairs={{0,16},{1,17},{2,18},{3,19},{4,20},{5,21},{6,22},{7,23},{8,24},{9,... | collective-permute-start | bytes 786440 | tf_op jit(solution)/shard_map/ppermute | solution.py:35
  472.0 19.6 %collective-permute-start.34 = (bf16[512,1024]{1,0:T(8,128)(2,1)S(1)}, bf16[512,1024]{1,0:T(8,128)(2,1)S(1)}, u32[]{:S(2)}, u32[]{:S(2)}) collective-permute-start(bf16[512,1024]{1,0:T(8,128)(2,1)S(1)} %add_convert_fusion), channel_id=1, source_target_pairs={{0,3},{1,2},{2,1},{3,0},{4,7},{5,6},{6,5},{7,4},{8,11},{9,10},{10,... | collective-permute-start | bytes 3145736 | tf_op jit(solution)/shard_map/ppermute | solution.py:35
  473.6 19.2 %collective-permute-start.31 = (bf16[512,1024]{1,0:T(8,128)(2,1)S(1)}, bf16[512,1024]{1,0:T(8,128)(2,1)S(1)}, u32[]{:S(2)}, u32[]{:S(2)}) collective-permute-start(bf16[512,1024]{1,0:T(8,128)(2,1)S(1)} %add_convert_fusion.1), channel_id=1, source_target_pairs={{0,48},{1,49},{2,50},{3,51},{4,52},{5,53},{6,54},{7,55},{8,56},{9,... | collective-permute-start | bytes 3145736 | tf_op jit(solution)/shard_map/ppermute | solution.py:35
  475.5 20.0 %collective-permute-start.28 = (bf16[512,1024]{1,0:T(8,128)(2,1)S(1)}, bf16[512,1024]{1,0:T(8,128)(2,1)S(1)}, u32[]{:S(2)}, u32[]{:S(2)}) collective-permute-start(bf16[512,1024]{1,0:T(8,128)(2,1)S(1)} %add_convert_fusion.2), channel_id=1, source_target_pairs={{0,12},{1,13},{2,14},{3,15},{4,8},{5,9},{6,10},{7,11},{8,4},{9,5},... | collective-permute-start | bytes 3145736 | tf_op jit(solution)/shard_map/ppermute | solution.py:35
  491.6 20.0 %collective-permute-start.26 = (f32[72,1024]{1,0:T(8,128)S(1)}, f32[72,1024]{1,0:T(8,128)S(1)}, u32[]{:S(2)}, u32[]{:S(2)}) collective-permute-start(f32[72,1024]{1,0:T(8,128)S(1)} %add.346), channel_id=1, source_target_pairs={{0,64},{64,0},{1,65},{65,1},{2,66},{66,2},{3,67},{67,3},{4,68},{68... | collective-permute-start | bytes 884744 | tf_op jit(solution)/shard_map/ppermute | solution.py:65
  (194 other events, 1343.9 us)
Sparse Core Ops, SparseCore 0:
  11.6 93.2 all-gather.1

commit v2 on v1

--- a/solution.py
+++ b/solution.py
@@ -1,3 +1,5 @@
+import functools
+
 import jax
 import jax.numpy as jnp
 from jax import lax
@@ -40,21 +42,63 @@
     return jnp.where(core == 0, tables[0], tables[1]) ^ me
 
 
-def natural_order(order):
-    return jnp.argmax(order[None, :] == jnp.arange(64, dtype=jnp.int32)[:, None], axis=1)
-
-
-def reorder(rows, order):
+def reorder_body(order_ref, rows_ref, out_ref):
+    for k in range(out_ref.shape[0]):
+        for r in range(64):
+            out_ref[k, r] = rows_ref[order_ref[k, r]]
+
+
+def reorder(rows, orders):
     blocks = rows.reshape(64, rows.shape[0] // 64, rows.shape[1])
-    return jnp.take(blocks, order, axis=0, mode="clip").reshape(rows.shape)
-
-
-def sum_everywhere(rows, core, part):
+    count = orders.shape[0]
+    out = pl.pallas_call(
+        reorder_body,
+        grid_spec=pltpu.PrefetchScalarGridSpec(
+            num_scalar_prefetch=1,
+            grid=(1,),
+            in_specs=[pl.BlockSpec(blocks.shape, lambda i, o: (0, 0, 0))],
+            out_specs=pl.BlockSpec((count, *blocks.shape), lambda i, o: (0, 0, 0, 0)),
+        ),
+        out_shape=jax.ShapeDtypeStruct((count, *blocks.shape), rows.dtype),
+        compiler_params=pltpu.CompilerParams(vmem_limit_bytes=32 * 1024 * 1024),
+    )(orders, blocks)
+    return [out[k].reshape(rows.shape) for k in range(count)]
+
+
+def collect_body(cuts, order_ref, *refs):
+    pieces, out_ref = refs[:-1], refs[-1]
+    count = len(pieces) // (len(cuts) - 1)
+    per = 64 // count
+    for k in range(len(cuts) - 1):
+        for r in range(64):
+            rows = pl.ds(pl.multiple_of(order_ref[k, r] * 32, 32), 32)
+            out_ref[rows, cuts[k] : cuts[k + 1]] = pieces[k * count + r // per][
+                (r % per) * 32 : (r % per + 1) * 32, :
+            ]
+
+
+def collect(pieces, cuts, orders):
+    flat = [piece for part in pieces for piece in part]
+    return pl.pallas_call(
+        functools.partial(collect_body, cuts),
+        grid_spec=pltpu.PrefetchScalarGridSpec(
+            num_scalar_prefetch=1,
+            grid=(1,),
+            in_specs=[pl.BlockSpec(a.shape, lambda i, o: (0, 0)) for a in flat],
+            out_specs=pl.BlockSpec((64 * 32, cuts[-1]), lambda i, o: (0, 0)),
+        ),
+        out_shape=jax.ShapeDtypeStruct((64 * 32, cuts[-1]), jnp.bfloat16),
+        compiler_params=pltpu.CompilerParams(vmem_limit_bytes=56 * 1024 * 1024),
+    )(orders, *flat)
+
+
+def half_of(rows, core):
     half = rows.shape[1] // 2
     own = lax.dynamic_slice_in_dim(rows, core * half, half, axis=1)
-    own = own + swap(lax.dynamic_slice_in_dim(rows, (1 - core) * half, half, axis=1))
-    for step in range(STEPS):
-        own = own + permute_step(own, part, step)
+    return own + swap(lax.dynamic_slice_in_dim(rows, (1 - core) * half, half, axis=1))
+
+
+def beside_other_half(own, core):
     other = swap(own)
     return jnp.concatenate(
         [jnp.where(core == 0, own, other), jnp.where(core == 0, other, own)], axis=1
@@ -63,6 +107,29 @@
 
 def swap(value):
     return lax.ppermute(value, "dp", [(0, 1), (1, 0)])
+
+
+def spanned(flips):
+    masks = [0]
+    for flip in flips:
+        masks += [mask ^ flip for mask in masks]
+    return masks
+
+
+def near_groups():
+    groups = []
+    for core in range(2):
+        masks = spanned(FLIPS[core])
+        for d in range(64):
+            if d == min(d ^ mask for mask in masks):
+                groups.append([64 * core + (d ^ mask) for mask in masks])
+    return groups
+
+
+def near_position(core, me):
+    low = (me & 1) | ((me >> 2) & 1) << 1 | ((me >> 4) & 1) << 2
+    high = ((me >> 1) & 1) | ((me >> 3) & 1) << 1 | ((me >> 5) & 1) << 2
+    return jnp.where(core == 0, low, high)
 
 
 def dot(left, right):
@@ -147,7 +214,7 @@
     count, width = out_ref.shape[0], rows.shape[1]
     half = width // 2
     out_ref[:, :width] = rows[:count]
-    out_ref[:, width:] = (
+    out_ref[:, width : width + half] = (
         dot_tn(half_picker(count, 0), rows[count:, :half])
         + dot_tn(half_picker(count, 1), rows[count:, half:])
     ).astype(jnp.bfloat16)
@@ -163,14 +230,10 @@
 
 def unpack(packed):
     count, width = packed.shape[0], packed.shape[1] * 2 // 3
-    block = count // 2
     return pl.pallas_call(
         unpack_body,
-        grid=(2,),
-        in_specs=[pl.BlockSpec((block, width * 3 // 2), lambda i: (i, 0))],
-        out_specs=pl.BlockSpec((block * 3 // 2, width), lambda i: (i, 0)),
         out_shape=jax.ShapeDtypeStruct((count * 3 // 2, width), jnp.bfloat16),
-        compiler_params=pltpu.CompilerParams(vmem_limit_bytes=32 * 1024 * 1024),
+        compiler_params=pltpu.CompilerParams(vmem_limit_bytes=56 * 1024 * 1024),
     )(packed)
 
 
@@ -197,14 +260,14 @@
         ],
         out_specs=pl.BlockSpec((block, width * 3 // 2), lambda i: (i, 0)),
         out_shape=jax.ShapeDtypeStruct((lines, width * 3 // 2), jnp.bfloat16),
-        compiler_params=pltpu.CompilerParams(vmem_limit_bytes=32 * 1024 * 1024),
+        compiler_params=pltpu.CompilerParams(vmem_limit_bytes=56 * 1024 * 1024),
     )(main, spare, rows)
 
 
 def combine_body(main_ref, spare_ref, lines_ref, out_ref):
     tokens, width = out_ref.shape
     half = width // 2
-    spare_lines = lines_ref[:, width:]
+    spare_lines = lines_ref[:, width : width + half]
     out_ref[:, :half] = dot(main_ref[...], lines_ref[:, :half]) + dot(
         spare_ref[:tokens], spare_lines
     )
@@ -213,91 +276,94 @@
     )
 
 
-def from_experts(main, spare, lines):
+def from_experts(main, spare, lines, width):
     return pl.pallas_call(
         combine_body,
-        out_shape=jax.ShapeDtypeStruct((main.shape[0], lines.shape[1] * 2 // 3), jnp.float32),
-        compiler_params=pltpu.CompilerParams(vmem_limit_bytes=32 * 1024 * 1024),
+        out_shape=jax.ShapeDtypeStruct((main.shape[0], width), jnp.float32),
+        compiler_params=pltpu.CompilerParams(vmem_limit_bytes=56 * 1024 * 1024),
     )(main, spare, lines)
 
 
-def out_body(core_ref, act_ref, own_ref, other_ref, out_ref):
+def out_body(core_ref, act_ref, own_ref, other_ref, extra_ref, out_ref):
     rows = dot(act_ref[0], own_ref[...]) + dot(act_ref[1], other_ref[...])
     pack_block(rows.astype(jnp.bfloat16), out_ref)
-
-
-def expert_results(acts, down_w, core):
+    out_ref[:, rows.shape[1] * 3 // 2 :] = extra_ref[...]
+
+
+def expert_results(acts, down_w, extra, core):
     _, count, units = acts.shape
-    width, block = down_w.shape[1], count // 2
+    width = down_w.shape[1]
+    shape = (count * 2 // 3, width * 3 // 2 + extra.shape[1])
     return pl.pallas_call(
         out_body,
         grid_spec=pltpu.PrefetchScalarGridSpec(
             num_scalar_prefetch=1,
-            grid=(2,),
+            grid=(1,),
             in_specs=[
-                pl.BlockSpec((2, block, units), lambda i, c: (0, i, 0)),
+                pl.BlockSpec((2, count, units), lambda i, c: (0, 0, 0)),
                 pl.BlockSpec((units, width), lambda i, c: (c[0], 0)),
                 pl.BlockSpec((units, width), lambda i, c: (1 - c[0], 0)),
+                pl.BlockSpec(extra.shape, lambda i, c: (0, 0)),
             ],
-            out_specs=pl.BlockSpec((block * 2 // 3, width * 3 // 2), lambda i, c: (i, 0)),
-        ),
-        out_shape=jax.ShapeDtypeStruct((count * 2 // 3, width * 3 // 2), jnp.bfloat16),
-        compiler_params=pltpu.CompilerParams(vmem_limit_bytes=40 * 1024 * 1024),
+            out_specs=pl.BlockSpec(shape, lambda i, c: (0, 0)),
+        ),
+        out_shape=jax.ShapeDtypeStruct(shape, jnp.bfloat16),
+        compiler_params=pltpu.CompilerParams(vmem_limit_bytes=56 * 1024 * 1024),
         cost_estimate=pl.CostEstimate(
             flops=4 * count * width * units, bytes_accessed=12 * 1024 * 1024, transcendentals=0
         ),
-    )(core[None].astype(jnp.int32), acts, down_w, down_w)
-
-
-def exchange(rows):
-    return lax.all_to_all(rows, "expert", split_axis=0, concat_axis=0, tiled=True)
+    )(core[None].astype(jnp.int32), acts, down_w, down_w, extra)
 
 
 def expert_body(
     core_ref, mine_ref, packed_ref, act_grad_ref, gate_w_ref, up_w_ref, router_ref,
-    back_ref, x_ref, gate_out_ref, up_out_ref, act_out_ref, logit_ref,
-    total, probs_ref, gate_ref, gate_grad_ref,
+    back_ref, x_out, gate_out_ref, up_out_ref, act_out_ref, logit_ref,
+    x_ref, total, probs_ref, gate_ref, gate_grad_ref, sem,
 ):
     f32, bf16 = jnp.float32, jnp.bfloat16
-    step = pl.program_id(1)
+    step = pl.program_id(0)
+    x_copy = pltpu.make_async_copy(x_ref, x_out, sem)
 
     @pl.when(step == 0)
     def _():
         unpack_body(packed_ref, x_ref)
+        x_copy.start()
         probs = softmax_rows(dot(x_ref[...], router_ref[...]))
         probs_ref[...] = probs
         gate_ref[...] = jnp.sum(probs * mine_ref[...], axis=1, keepdims=True)
         gate_grad_ref[...] = jnp.zeros_like(gate_grad_ref)
-
-    x = x_ref[...]
-    gate_w, up_w, gate = gate_w_ref[...], up_w_ref[...], gate_ref[...]
-    gate_pre, up_pre = dot(x, gate_w), dot(x, up_w)
-    plain = act_grad_ref[...]
-    sigmoid = 1.0 / (1.0 + jnp.exp(-gate_pre))
-    silu = gate_pre * sigmoid
-    act = silu * up_pre
-    gate_grad_ref[...] += jnp.sum(act * plain, axis=1, keepdims=True)
-    act_grad = gate * plain
-    gate_pre_grad = (act_grad * up_pre * sigmoid * (1.0 + gate_pre * (1.0 - sigmoid))).astype(bf16)
-    up_pre_grad = (act_grad * silu).astype(bf16)
-    gate_out_ref[0] = gate_pre_grad
-    up_out_ref[0] = up_pre_grad
-    act_out_ref[0] = (gate * act).astype(bf16)
-    part = dot_nt(gate_pre_grad, gate_w) + dot_nt(up_pre_grad, up_w)
-
-    @pl.when(step == 0)
+        total[...] = jnp.zeros_like(total)
+
+    gate_w, up_w = gate_w_ref[...], up_w_ref[...]
+    size = x_ref.shape[0] // 3
+    for k in range(3):
+        rows = pl.ds(k * size, size)
+        x, gate = x_ref[rows, :], gate_ref[rows, :]
+        gate_pre, up_pre = dot(x, gate_w), dot(x, up_w)
+        plain = act_grad_ref[rows, :].astype(f32)
+        sigmoid = 1.0 / (1.0 + jnp.exp(-gate_pre))
+        silu = gate_pre * sigmoid
+        act = silu * up_pre
+        gate_grad = jnp.sum(act * plain, axis=1, keepdims=True)
+        act_grad = gate * plain
+        gate_pre_grad = (act_grad * up_pre * sigmoid * (1.0 + gate_pre * (1.0 - sigmoid))).astype(
+            bf16
+        )
+        up_pre_grad = (act_grad * silu).astype(bf16)
+        gate_out_ref[0, rows, :] = gate_pre_grad
+        up_out_ref[0, rows, :] = up_pre_grad
+        act_out_ref[0, rows, :] = (gate * act).astype(bf16)
+        part = dot_nt(gate_pre_grad, gate_w) + dot_nt(up_pre_grad, up_w)
+
+        gate_grad_ref[rows, :] += gate_grad
+        total[rows, :] += part
+
+    @pl.when(step == pl.num_programs(0) - 1)
     def _():
-        total[...] = part
-
-    @pl.when(step > 0)
-    def _():
-        total[...] += part
-
-    @pl.when(step == pl.num_programs(1) - 1)
-    def _():
-        logit = (gate_grad_ref[...] * gate * (mine_ref[...] - probs_ref[...])).astype(bf16)
+        logit = (gate_grad_ref[...] * gate_ref[...] * (mine_ref[...] - probs_ref[...])).astype(bf16)
         logit_ref[...] = logit
         pack_block((total[...] + dot_nt(logit, router_ref[...])).astype(bf16), back_ref)
+        x_copy.wait()
 
 
 def expert_rows(packed, plain_act_grad, gate_w, up_w, router, core, me):
@@ -305,38 +371,38 @@
     lines = packed.shape[0]
     width, units = gate_w.shape
     count, experts = lines * 3 // 2, router.shape[1]
-    tiles = 4
-    block, tile, cut = count // 2, units // tiles, tiles // 2
+    tile = units // 4
     mine = (jnp.arange(experts, dtype=jnp.int32) == me).astype(f32)[None, :]
     halves = jax.ShapeDtypeStruct((2, count, units // 2), bf16)
-    half_spec = pl.BlockSpec((1, block, tile), lambda i, j, c: ((j // cut + c[0]) % 2, i, j % cut))
-    packed_spec = pl.BlockSpec((lines // 2, width * 3 // 2), lambda i, j, c: (i, 0))
+    half_spec = pl.BlockSpec((1, count, tile), lambda j, c: ((j // 2 + c[0]) % 2, 0, j % 2))
     return pl.pallas_call(
         expert_body,
         grid_spec=pltpu.PrefetchScalarGridSpec(
             num_scalar_prefetch=1,
-            grid=(2, tiles),
+            grid=(4,),
             in_specs=[
-                pl.BlockSpec((1, experts), lambda i, j, c: (0, 0)),
-                packed_spec,
-                pl.BlockSpec((block, tile), lambda i, j, c: (i, j)),
-                pl.BlockSpec((width, tile), lambda i, j, c: (0, j)),
-                pl.BlockSpec((width, tile), lambda i, j, c: (0, j)),
-                pl.BlockSpec((width, experts), lambda i, j, c: (0, 0)),
+                pl.BlockSpec((1, experts), lambda j, c: (0, 0)),
+                pl.BlockSpec(packed.shape, lambda j, c: (0, 0)),
+                pl.BlockSpec((count, tile), lambda j, c: (0, j)),
+                pl.BlockSpec((width, tile), lambda j, c: (0, j)),
+                pl.BlockSpec((width, tile), lambda j, c: (0, j)),
+                pl.BlockSpec((width, experts), lambda j, c: (0, 0)),
             ],
             out_specs=[
-                packed_spec,
-                pl.BlockSpec((block, width), lambda i, j, c: (i, 0)),
+                pl.BlockSpec(packed.shape, lambda j, c: (0, 0)),
+                pl.BlockSpec(memory_space=pl.ANY),
                 half_spec,
                 half_spec,
                 half_spec,
-                pl.BlockSpec((block, experts), lambda i, j, c: (i, 0)),
+                pl.BlockSpec((count, experts), lambda j, c: (0, 0)),
             ],
             scratch_shapes=[
-                pltpu.VMEM((block, width), f32),
-                pltpu.VMEM((block, experts), f32),
-                pltpu.VMEM((block, 1), f32),
-                pltpu.VMEM((block, 1), f32),
+                pltpu.VMEM((count, width), bf16),
+                pltpu.VMEM((count, width), f32),
+                pltpu.VMEM((count, experts), f32),
+                pltpu.VMEM((count, 1), f32),
+                pltpu.VMEM((count, 1), f32),
+                pltpu.SemaphoreType.DMA,
             ],
         ),
         out_shape=[
@@ -347,22 +413,157 @@
             halves,
             jax.ShapeDtypeStruct((count, experts), bf16),
         ],
-        compiler_params=pltpu.CompilerParams(vmem_limit_bytes=48 * 1024 * 1024),
+        compiler_params=pltpu.CompilerParams(vmem_limit_bytes=60 * 1024 * 1024),
         cost_estimate=pl.CostEstimate(
-            flops=8 * count * width * units, bytes_accessed=36 * 1024 * 1024, transcendentals=count * units
+            flops=8 * count * width * units, bytes_accessed=24 * 1024 * 1024, transcendentals=count * units
         ),
     )(core[None].astype(jnp.int32), mine, packed, plain_act_grad, gate_w, up_w, router)
 
 
-def output_body(core_ref, heads_ref, weight_ref, inputs_ref, own_ref, other_ref):
-    count, half = own_ref.shape
-    weight = weight_ref[...].reshape(half, half)
-    first = pl.multiple_of(core_ref[0] * count, count)
-    second = pl.multiple_of((1 - core_ref[0]) * count, count)
-    other_ref[...] = dot(heads_ref[pl.ds(second, count), :], weight).astype(jnp.bfloat16)
-    own_ref[...] = dot(heads_ref[pl.ds(first, count), :], weight) + inputs_ref[...].astype(
-        jnp.float32
-    )
+PARTS = ((0, 384), (384, 768), (768, 1024))
+OFFSETS = (0, 1408, 2816, 4096)
+
+
+def part_sums(part, left, low, heads, grad, got):
+    start, stop = PARTS[part]
+    blocks = left.shape[0] // 32
+    half = grad.shape[1] // 2
+    main = dot(left, low).reshape(blocks, 32, low.shape[1])
+    sides = [
+        dot(heads, grad[:, h * half + start : h * half + stop]).reshape(blocks, 16, stop - start)
+        for h in range(2)
+    ]
+    for g in got:
+        main = main + g[:, :, : low.shape[1]].astype(jnp.float32)
+        sides = [
+            sides[h] + g[:, 16 * h : 16 * h + 16, low.shape[1] :].astype(jnp.float32)
+            for h in range(2)
+        ]
+    return main, sides
+
+
+def sent_body(count, *refs):
+    lefts, lows, heads, grad = refs[:3], refs[3:6], refs[6:9], refs[9][...]
+    got, outs = refs[10 : 10 + 3 * count], refs[10 + 3 * count :]
+    for k in range(3):
+        main, sides = part_sums(
+            k, lefts[k][...], lows[k][...], heads[k][...], grad,
+            [g[...] for g in got[k * count : (k + 1) * count]],
+        )
+        width = main.shape[2]
+        outs[k][:, :, :width] = main.astype(jnp.bfloat16)
+        for h in range(2):
+            outs[k][:, 16 * h : 16 * h + 16, width:] = sides[h].astype(jnp.bfloat16)
+
+
+def sent_pieces(step, lefts, lows, heads, grad, got):
+    blocks = 1 << step
+    chunk = min(blocks, 8)
+    first = blocks // chunk
+    count = len(got[0])
+    ahead = lambda i: (first + i, 0)
+    ahead3 = lambda i: (first + i, 0, 0)
+    fixed = lambda i: (0, 0)
+    columns = [OFFSETS[k + 1] - OFFSETS[k] for k in range(3)]
+    return pl.pallas_call(
+        functools.partial(sent_body, count),
+        grid=(blocks // chunk,),
+        in_specs=[pl.BlockSpec((chunk * 32, a.shape[1]), ahead) for a in lefts]
+        + [pl.BlockSpec(a.shape, fixed) for a in lows]
+        + [pl.BlockSpec((chunk * 16, a.shape[1]), ahead) for a in heads]
+        + [pl.BlockSpec(grad.shape, fixed)]
+        + [pl.BlockSpec((chunk, 32, columns[k]), ahead3) for k in range(3) for _ in range(count)],
+        out_specs=[pl.BlockSpec((chunk, 32, c), lambda i: (i, 0, 0)) for c in columns],
+        out_shape=[jax.ShapeDtypeStruct((blocks, 32, c), jnp.bfloat16) for c in columns],
+        compiler_params=pltpu.CompilerParams(
+            vmem_limit_bytes=(32 if step == 5 else 56) * 1024 * 1024
+        ),
+    )(*lefts, *lows, *heads, grad, *(g for k in range(3) for g in got[k]))
+
+
+def near_body(place_ref, left_ref, *refs):
+    lows, heads_ref, grad_ref, got, out_ref = refs[:3], refs[3], refs[4], refs[5:14], refs[14]
+    for k in range(3):
+        main, sides = part_sums(
+            k, left_ref[...], lows[k][...], heads_ref[...], grad_ref[...],
+            [g[...] for g in got[3 * k : 3 * k + 3]],
+        )
+        width, start, stop = main.shape[2], OFFSETS[k], OFFSETS[k + 1]
+        for r in range(8):
+            place = place_ref[0] ^ r
+            out_ref[place, :, start : start + width] = main[r].astype(jnp.bfloat16)
+            for h in range(2):
+                out_ref[place, 16 * h : 16 * h + 16, start + width : stop] = sides[h][r].astype(
+                    jnp.bfloat16
+                )
+
+
+def near_pieces(place, left, lows, heads, grad, got):
+    return pl.pallas_call(
+        near_body,
+        grid_spec=pltpu.PrefetchScalarGridSpec(
+            num_scalar_prefetch=1,
+            grid=(1,),
+            in_specs=[pl.BlockSpec((8 * 32, left.shape[1]), lambda i, c: (0, 0))]
+            + [pl.BlockSpec(a.shape, lambda i, c: (0, 0)) for a in lows]
+            + [
+                pl.BlockSpec((8 * 16, heads.shape[1]), lambda i, c: (0, 0)),
+                pl.BlockSpec(grad.shape, lambda i, c: (0, 0)),
+            ]
+            + [
+                pl.BlockSpec((8, 32, g.shape[2]), lambda i, c: (0, 0, 0))
+                for k in range(3)
+                for g in got[k]
+            ],
+            out_specs=pl.BlockSpec((8, 32, OFFSETS[3]), lambda i, c: (0, 0, 0)),
+        ),
+        out_shape=jax.ShapeDtypeStruct((8, 32, OFFSETS[3]), jnp.bfloat16),
+        compiler_params=pltpu.CompilerParams(vmem_limit_bytes=56 * 1024 * 1024),
+    )(place[None].astype(jnp.int32), left, *lows, heads, grad, *(g for k in range(3) for g in got[k]))
+
+
+def total_body(near_ref, *outs):
+    out_ref = outs[3]
+    half = out_ref.shape[1] // 2
+    for k in range(3):
+        start, stop = OFFSETS[k], OFFSETS[k + 1]
+        total = near_ref[0, :, start:stop].astype(jnp.float32)
+        for r in range(1, near_ref.shape[0]):
+            total = total + near_ref[r, :, start:stop].astype(jnp.float32)
+        outs[k][...] = total[:, :half]
+        for h in range(2):
+            out_ref[:, h * half + PARTS[k][0] : h * half + PARTS[k][1]] = total[
+                16 * h : 16 * h + 16, half:
+            ]
+
+
+def near_total(near):
+    rows, half = near.shape[1], 1024
+    return pl.pallas_call(
+        total_body,
+        out_shape=[jax.ShapeDtypeStruct((rows, half), jnp.float32)] * 3
+        + [jax.ShapeDtypeStruct((rows // 2, 2 * half), jnp.float32)],
+        compiler_params=pltpu.CompilerParams(vmem_limit_bytes=56 * 1024 * 1024),
+    )(near)
+
+
+def exchange(rows):
+    return lax.all_to_all(rows, "expert", split_axis=0, concat_axis=0, tiled=True)
+
+
+def own_and_other(core_ref, total, own_ref, other_ref):
+    count = own_ref.shape[0]
+    own_ref[...] = total[pl.ds(pl.multiple_of(core_ref[0] * count, count), count), :]
+    other_ref[...] = total[
+        pl.ds(pl.multiple_of((1 - core_ref[0]) * count, count), count), :
+    ].astype(other_ref.dtype)
+
+
+def output_body(core_ref, heads_ref, weight_ref, inputs_ref, own_ref, other_ref, total):
+    half = own_ref.shape[1]
+    total[...] = dot(heads_ref[...], weight_ref[...].reshape(half, half))
+    own_and_other(core_ref, total, own_ref, other_ref)
+    own_ref[...] += inputs_ref[...].astype(jnp.float32)
 
 
 def output_shares(heads, stacked, inputs, core):
@@ -379,12 +580,13 @@
                 pl.BlockSpec((tokens, half), lambda h, c: (0, h)),
             ],
             out_specs=[pl.BlockSpec((tokens, half), lambda h, c: (0, h))] * 2,
+            scratch_shapes=[pltpu.VMEM((2 * tokens, half), jnp.float32)],
         ),
         out_shape=[
             jax.ShapeDtypeStruct((tokens, width), jnp.float32),
             jax.ShapeDtypeStruct((tokens, width), jnp.bfloat16),
         ],
-        compiler_params=pltpu.CompilerParams(vmem_limit_bytes=32 * 1024 * 1024),
+        compiler_params=pltpu.CompilerParams(vmem_limit_bytes=56 * 1024 * 1024),
     )(core[None].astype(jnp.int32), heads, stacked, inputs)
 
 
@@ -414,24 +616,28 @@
         out_specs=pl.BlockSpec((tokens, half), lambda h: (0, 0)),
         out_shape=jax.ShapeDtypeStruct((tokens, half), jnp.bfloat16),
         scratch_shapes=[pltpu.VMEM((tokens, half), jnp.float32)],
-        compiler_params=pltpu.CompilerParams(vmem_limit_bytes=32 * 1024 * 1024),
+        compiler_params=pltpu.CompilerParams(vmem_limit_bytes=56 * 1024 * 1024),
     )(grad, stacked)
 
 
-def share_body(core_ref, lows_ref, both_w_ref, value_w_ref, own_ref, other_ref):
-    tokens = own_ref.shape[0]
-    middle = both_w_ref.shape[1]
-    first = pl.ds(pl.multiple_of(core_ref[0] * tokens, tokens), tokens)
-    second = pl.ds(pl.multiple_of((1 - core_ref[0]) * tokens, tokens), tokens)
-    for rows, out_ref in ((second, other_ref), (first, own_ref)):
-        share = dot_nt(lows_ref[rows, :middle], both_w_ref[...]) + dot_nt(
-            lows_ref[rows, middle:], value_w_ref[...]
-        )
-        out_ref[...] = share.astype(out_ref.dtype)
-
-
-def input_shares(lows, both_w, value_w, core):
-    tokens, width = lows.shape[0] // 2, both_w.shape[0]
+def share_body(
+    core_ref, query_ref, key_ref, value_ref, scaled_ref, both_w_ref, value_w_ref,
+    own_ref, other_ref, gain_ref, total,
+):
+    middle = both_w_ref.shape[1] // 2
+    total[...] = (
+        dot_nt(query_ref[...], both_w_ref[:, :middle])
+        + dot_nt(key_ref[...], both_w_ref[:, middle:])
+        + dot_nt(value_ref[...], value_w_ref[...])
+    )
+    own_and_other(core_ref, total, own_ref, other_ref)
+    gain_ref[...] = jnp.sum(
+        total[...] * scaled_ref[...].astype(jnp.float32), axis=0, keepdims=True
+    )
+
+
+def input_shares(lows, scaled, both_w, value_w, core):
+    tokens, width = lows[0].shape[0] // 2, both_w.shape[0]
     half, tile = value_w.shape[1] // 2, width // 8
     return pl.pallas_call(
         share_body,
@@ -439,21 +645,25 @@
             num_scalar_prefetch=1,
             grid=(8,),
             in_specs=[
-                pl.BlockSpec(lows.shape, lambda i, c: (0, 0)),
+                *(pl.BlockSpec(a.shape, lambda i, c: (0, 0)) for a in lows),
+                pl.BlockSpec((2 * tokens, tile), lambda i, c: (0, i)),
                 pl.BlockSpec((tile, width), lambda i, c: (i, 0)),
                 pl.BlockSpec((tile, half), lambda i, c: (i, 0)),
             ],
-            out_specs=[pl.BlockSpec((tokens, tile), lambda i, c: (0, i))] * 2,
+            out_specs=[pl.BlockSpec((tokens, tile), lambda i, c: (0, i))] * 2
+            + [pl.BlockSpec((1, tile), lambda i, c: (0, i))],
+            scratch_shapes=[pltpu.VMEM((2 * tokens, tile), jnp.float32)],
         ),
         out_shape=[
             jax.ShapeDtypeStruct((tokens, width), jnp.float32),
             jax.ShapeDtypeStruct((tokens, width), jnp.bfloat16),
+            jax.ShapeDtypeStruct((1, width), jnp.float32),
         ],
-        compiler_params=pltpu.CompilerParams(vmem_limit_bytes=32 * 1024 * 1024),
+        compiler_params=pltpu.CompilerParams(vmem_limit_bytes=56 * 1024 * 1024),
         cost_estimate=pl.CostEstimate(
-            flops=24 * 1000 * 1000 * 1000, bytes_accessed=16 * 1024 * 1024, transcendentals=0
-        ),
-    )(core[None].astype(jnp.int32), lows, both_w, value_w)
+            flops=4 * 1000 * 1000 * 1000, bytes_accessed=16 * 1024 * 1024, transcendentals=0
+        ),
+    )(core[None].astype(jnp.int32), *lows, scaled, both_w, value_w)
 
 
 def shards(
@@ -509,8 +719,7 @@
         pieces[k].append(permute_step(pieces[k][0], k, 4))
     for k in range(3):
         pieces[k] += [permute_step(piece, k, 5) for piece in pieces[k]]
-    orders = [relative_order(core, me, part) for part in range(3)]
-    inverses = [natural_order(order) for order in orders]
+    orders = jnp.stack([relative_order(core, me, part) for part in range(3)])
 
     assigned = token_assignments[0]
     expert_iota = jnp.arange(experts, dtype=jnp.int32)
@@ -552,7 +761,8 @@
     factor_in = rms_factor(inputs)
     normed_in = (inputs * factor_in * mixing_scale_factor).astype(bf16)
     normed_t = whole_row(normed_in).T
-    normed_rel = [reorder(normed_t, order) for order in orders]
+    scaled_in = whole_row((inputs * factor_in).astype(bf16))
+    normed_rel = reorder(normed_t, orders)
 
     def project(left, pieces):
         size = width // len(pieces)
@@ -563,7 +773,7 @@
     value_low = dot_tn(normed_t, value_output[:, :half_width]).astype(bf16).reshape(head_shape)
     grad_top_low = block_result_cotangent[0]
     send_grads, *_ = lax.optimization_barrier(
-        (to_experts(main, spare, grad_top_low), *(pieces[k][-1] for k in range(3)))
+        (to_experts(main, spare, grad_top_low), *(pieces[k][3] for k in range(3)))
     )
     arrived_grads = exchange(send_grads)
     query_sq, key_sq = lax.psum(
@@ -594,51 +804,55 @@
 
     arrived = exchange(to_experts(main, spare, normed_moe))
     *late_pieces, _ = lax.optimization_barrier((*pieces, normed_moe))
-    both_w = jnp.concatenate(
-        [reorder(jnp.concatenate(late_pieces[k], axis=0), inverses[k]) for k in range(3)], axis=1
-    )
-    both_w, arrived = lax.optimization_barrier((both_w, arrived))
+    both_w = collect(late_pieces, cuts, orders)
+    mixed_rel = reorder(mixed_heads.T, orders)
+    both_w, mixed_rel, arrived = lax.optimization_barrier((both_w, mixed_rel, arrived))
     gate_w, up_w, down_w = (
         specialist_switch_tensor[0],
         specialist_widen_tensor[0],
         specialist_shrink_tensor[0],
     )
     top_rows = unpack(arrived_grads)
-    plain_act_grad = dot_nt(top_rows, down_w)
+    plain_act_grad = dot_nt(top_rows, down_w).astype(bf16)
     row_grad, rows_in, gate_pre_grad, up_pre_grad, gated_act, logit_grad = expert_rows(
         arrived, plain_act_grad, gate_w, up_w, dispatcher_projection, core, me
     )
     returned_grads = exchange(row_grad)
-    send_out, returned_grads = lax.optimization_barrier(
-        (expert_results(gated_act, down_w, core), returned_grads)
+
+    own_counts = jnp.where(
+        (jnp.arange(2)[:, None, None] == core) & (expert_iota[None, :, None] == me),
+        sent_counts[None, None, :],
+        0,
+    ).astype(f32)
+    early = half_of(
+        jnp.concatenate(
+            [dot_tn(logit_grad, rows_in), own_counts.reshape(2 * experts * experts // width, width)]
+        ),
+        core,
+    )
+    small_rows, small_cols = early.shape[0], half_width // 64
+    extra = early.reshape(small_rows, 64, small_cols).transpose(1, 0, 2).reshape(64 * 8, -1)
+    extra = jnp.pad(extra.astype(bf16), ((0, 0), (0, 256 - extra.shape[1])))
+    unit_grads = [
+        swap(dot_tn(left, right).astype(bf16))
+        for left, right in (
+            (rows_in, gate_pre_grad[1]),
+            (rows_in, up_pre_grad[1]),
+            (gated_act[1], top_rows),
+        )
+    ]
+    send_out, returned_grads, unit_grads = lax.optimization_barrier(
+        (expert_results(gated_act, down_w, extra, core), returned_grads, unit_grads)
     )
     returned = exchange(send_out)
 
-    def summed(left, right):
-        return left + swap(right.astype(bf16)).astype(f32)
-
-    gate_weight_grad = summed(dot_tn(rows_in, gate_pre_grad[0]), dot_tn(rows_in, gate_pre_grad[1]))
-    up_weight_grad = summed(dot_tn(rows_in, up_pre_grad[0]), dot_tn(rows_in, up_pre_grad[1]))
-    down_weight_grad = summed(dot_tn(gated_act[0], top_rows), dot_tn(gated_act[1], top_rows))
-
-    moe_in_grad = from_experts(main, spare, returned_grads)
+    moe_in_grad = from_experts(main, spare, returned_grads, width)
     hidden_norm_grad, moe_gain_local = norm_back(
         moe_in_grad, hidden, factor_moe, specialist_scale_factor
     )
     hidden_grad = grad_top_low.astype(f32) + hidden_norm_grad
     grad_full = whole_row(hidden_grad.astype(bf16))
     mixed_grad = heads_grad(grad_full, stacked_output).reshape(head_shape)
-    mixed_rel = reorder(mixed_heads.T, orders[0])
-    output_rows, output_got = width // 128, []
-    for step in reversed(range(STEPS)):
-        low, high = 1 << step, 2 << step
-        piece = dot(mixed_rel[low * output_rows : high * output_rows], grad_full)
-        for g in output_got:
-            piece = piece + g[low * output_rows : high * output_rows].astype(f32)
-        output_got.append(permute_step(piece.astype(bf16), 0, step))
-    output_weight_grad = dot(mixed_rel[:output_rows], grad_full)
-    for g in output_got:
-        output_weight_grad = output_weight_grad + g[:output_rows].astype(f32)
     prob_grad_att = jnp.einsum("qhd,khd->hqk", mixed_grad, value_low, preferred_element_type=f32)
     score_grad = (
         attn_probs * (prob_grad_att - jnp.sum(attn_probs * prob_grad_att, axis=-1, keepdims=True))
@@ -675,58 +889,64 @@
     )
     lows = (query_low, key_low, value_proj_low)
 
-    def left_of(k, low, high):
-        return normed_rel[k][low * (width // 64) : high * (width // 64)]
-
-    sent = [dot(left_of(k, 32, 64), lows[k]).astype(bf16) for k in range(3)]
-    *sent, share_lows, returned = lax.optimization_barrier((*sent, lows, returned))
-    share_own, share_other = input_shares(
-        jnp.concatenate(share_lows, axis=1), both_w, value_output, core
-    )
-    got = [[permute_step(sent[k], k, 5)] for k in range(3)]
-    rows = width // 64
-    for step in (4, 3):
-        low, high = 1 << step, 2 << step
+    got = [[], [], []]
+    for step in (5, 4, 3):
+        sent = sent_pieces(step, normed_rel, lows, mixed_rel, grad_full, got)
+        if step == 5:
+            sent, unit_grads, share_lows = lax.optimization_barrier((sent, unit_grads, lows))
         for k in range(3):
-            piece = dot(left_of(k, low, high), lows[k])
-            for g in got[k]:
-                piece = piece + g[low * rows : high * rows].astype(f32)
-            got[k].append(permute_step(piece.astype(bf16), k, step))
-    near = [sum(g[: 8 * rows].astype(f32) for g in got[k]) for k in range(3)]
-    projection_grads, output_weight_grad = lax.optimization_barrier(
-        (jnp.concatenate(near, axis=1), output_weight_grad)
-    )
-    low_all = jnp.concatenate(lows, axis=1)
-    for step in (2, 1, 0):
-        low, high = 1 << step, 2 << step
-        piece = dot(left_of(0, low, high), low_all) + projection_grads[low * rows :]
-        projection_grads = projection_grads[: low * rows] + permute_step(
-            piece.astype(bf16), 0, step
-        ).astype(f32)
-    projection_grads = projection_grads + dot(left_of(0, 0, 1), low_all)
-    block_output = hidden + from_experts(main, spare, returned)
-    normed_in_grad = share_own + swap(share_other).astype(f32)
-    input_norm_grad, attn_gain_local = norm_back(
+            got[k].append(permute_step(sent[k], k, step))
+        if step == 5:
+            gate_weight_grad = dot_tn(rows_in, gate_pre_grad[0]) + unit_grads[0].astype(f32)
+            up_weight_grad = dot_tn(rows_in, up_pre_grad[0]) + unit_grads[1].astype(f32)
+            down_weight_grad = dot_tn(gated_act[0], top_rows) + unit_grads[2].astype(f32)
+            shares = input_shares(share_lows, scaled_in, both_w, value_output, core)
+            attn_gain_local = shares[2][0]
+            got, returned, gate_weight_grad, up_weight_grad, down_weight_grad, shares = (
+                lax.optimization_barrier(
+                    (got, returned, gate_weight_grad, up_weight_grad, down_weight_grad, shares[:2])
+                )
+            )
+        if step == 4:
+            block_output = hidden + from_experts(main, spare, returned, width)
+            got, shares, block_output = lax.optimization_barrier((got, shares, block_output))
+    near = lax.all_to_all(
+        near_pieces(near_position(core, me), normed_rel[0], lows, mixed_rel[0], grad_full, got),
+        BOTH,
+        split_axis=0,
+        concat_axis=0,
+        tiled=True,
+        axis_index_groups=near_groups(),
+    )
+    query_weight_grad, key_weight_grad, value_weight_grad, output_weight_grad = near_total(near)
+    normed_in_grad = shares[0] + swap(shares[1]).astype(f32)
+    input_norm_grad, _ = norm_back(
         normed_in_grad, inputs, factor_in, mixing_scale_factor
     )
     input_grad = hidden_grad + input_norm_grad
 
-    own_counts = jnp.where(
-        (jnp.arange(2)[:, None, None] == core) & (expert_iota[None, :, None] == me),
-        sent_counts[None, None, :],
-        0,
-    ).astype(f32)
-    totals = sum_everywhere(
-        jnp.concatenate(
-            [
-                dot_tn(logit_grad, rows_in),
-                own_counts.reshape(2 * experts * experts // width, width),
-                jnp.stack([attn_gain_local, query_gain_local, key_gain_local, moe_gain_local]),
-            ]
-        ),
-        core,
-        1,
-    )
+    gains = half_of(
+        jnp.stack([attn_gain_local, query_gain_local, key_gain_local, moe_gain_local]), core
+    )
+    early = jnp.sum(
+        returned[:, width * 3 // 2 : width * 3 // 2 + small_rows * small_cols // 8]
+        .reshape(64, small_rows * small_cols)
+        .astype(f32),
+        axis=0,
+    )
+    small = jnp.concatenate([early, gains.reshape(-1)])
+    small = jnp.pad(small, (0, 6144 - small.shape[0])).reshape(8, 768)
+    small = lax.all_gather(small, "expert", axis=0, tiled=True).reshape(64, 6144)
+    early = (
+        small[:, : small_rows * small_cols]
+        .reshape(64, small_rows, small_cols)
+        .transpose(1, 0, 2)
+        .reshape(small_rows, half_width)
+    )
+    gains = jnp.sum(
+        small[:, small_rows * small_cols : small_rows * small_cols + 4 * half_width], axis=0
+    ).reshape(4, half_width)
+    totals = beside_other_half(jnp.concatenate([early, gains]), core)
     router_weight_grad, all_counts, gains = totals[:experts].T, totals[experts:-4], totals[-4:]
     got_counts = jnp.sum(
         jnp.where(
@@ -740,9 +960,9 @@
         block_output[None],
         input_grad[None],
         gains[0],
-        projection_grads[:, :half_width],
-        projection_grads[:, half_width : 2 * half_width],
-        projection_grads[:, 2 * half_width :],
+        query_weight_grad,
+        key_weight_grad,
+        value_weight_grad,
         output_weight_grad,
         gains[1],
         gains[2],

time: 555 us -> 493 us (0.89)
  the two profiles are of different devices: /device:TPU:0 before, /device:TPU:5 now
where the time goes in v2:
time: 493 us; the launch traced here: 484 us
  waiting for transfers between devices  109 us (22%)
  Pallas kernels  106 us (22%)
  starting transfers between devices  94.2 us (19%)
  matrix products  59.4 us (12%)
  other arithmetic  49.6 us (10%)
  local copies, waits for them, and re-layouts  39 us (8%)
  between operations  16 us (3%)
  blocking collectives  11.4 us (2%)
    ppermute x24, waiting for transfers between devices, permute_step(): return lax.ppermute(value, BOTH, pairs)  71.9 us
    dot_general x20, matrix products, dot_tn(): lax.dot_general(left, right, (((0,), (0,)), ((), ())), preferred_element_...  41.7 us
    all_to_all x4, starting transfers between devices, exchange(): lax.all_to_all(rows, 'expert', split_axis=0, concat_axis=0, tiled=True)  35.7 us
    all_to_all x4, waiting for transfers between devices, exchange(): lax.all_to_all(rows, 'expert', split_axis=0, concat_axis=0, tiled=True)  30.5 us
    ppermute x24, starting transfers between devices, permute_step(): return lax.ppermute(value, BOTH, pairs)  29.4 us
    pallas_call x1, Pallas kernels, expert_rows(): pl.pallas_call(expert_body, grid_spec=pltpu.PrefetchScalarGridSpec(num_sc...  25.3 us
    ppermute x11, starting transfers between devices, swap(): return lax.ppermute(value, 'dp', [(0, 1), (1, 0)])  24 us
    pallas_call x3, Pallas kernels, sent_pieces(): pl.pallas_call(functools.partial(sent_body, count), grid=(blocks // chunk...  14.4 us
  transfers between devices with their start and end apart: 42, of which 21 were waited for; matrix products, arithmetic and copies ran while one was open for 28% of the time, Pallas kernels for 16%

profile of v2, /device:TPU:5, one launch (start us, length us, event | category | flops | bytes accessed | tf_op | source)
XLA Modules:
  0.0 483.9 jit_solution(18342017109277850526)
XLA Ops:
  64.9 8.0 %collective-permute-done.13.refs_9_ = bf16[512,640]{1,0:T(8,128)(2,1)S(1)} collective-permute-done((bf16[512,640]{1,0:T(8,128)(2,1)S(1)}, bf16[512,640]{1,0:T(8,128)(2,1)S(1)}, u32[]{:S(2)}, u32[]{:S(2)}) %collective-permute-start.13) | collective-permute-done | bytes 655392 | tf_op jit(solution)/shard_map/ppermute | solution.py:37
  80.0 14.0 %collective-permute-done.11.refs_7_ = bf16[512,640]{1,0:T(8,128)(2,1)S(1)} collective-permute-done((bf16[512,640]{1,0:T(8,128)(2,1)S(1)}, bf16[512,640]{1,0:T(8,128)(2,1)S(1)}, u32[]{:S(2)}, u32[]{:S(2)}) %collective-permute-start.11) | collective-permute-done | bytes 655392 | tf_op jit(solution)/shard_map/ppermute | solution.py:37
  104.7 8.7 %all-reduce.3 = (f32[256]{0:T(256)S(1)}, f32[256]{0:T(256)S(1)}) all-reduce(f32[256]{0:T(256)S(1)} %get-tuple-element.221, f32[256]{0:T(256)S(1)} %get-tuple-element.220), channel_id=1, replica_groups=mesh['dp'=2,'expert'=64] {'dp'}, use_global_device_ids=true, to_apply=%region_2.3 | all-reduce | flops 512 | bytes 4096 | tf_op jit(solution)/shard_map/psum | solution.py:779
  117.6 7.8 %all-to-all-start.1 = ((bf16[64,8,3072]{2,1,0:T(8,128)(2,1)}), bf16[64,8,3072]{2,1,0:T(8,128)(2,1)}, u32[]{:S(2)}, u32[]{:S(2)}) async-start(bf16[64,8,3072]{2,1,0:T(8,128)(2,1)} %bitcast.227), calls=%async_computation.1 | async-start | bytes 6291456 | tf_op jit(solution)/shard_map/all_to_all | solution.py:551
  155.8 9.9 %all-to-all-done.1 = bf16[64,8,3072]{2,1,0:T(8,128)(2,1)} async-done(((bf16[64,8,3072]{2,1,0:T(8,128)(2,1)}), bf16[64,8,3072]{2,1,0:T(8,128)(2,1)}, u32[]{:S(2)}, u32[]{:S(2)}) %all-to-all-start.1) | async-done | bytes 3145760 | tf_op jit(solution)/shard_map/all_to_all | solution.py:551
  165.7 8.3 %all-to-all-start = ((bf16[64,8,3072]{2,1,0:T(8,128)(2,1)}), bf16[64,8,3072]{2,1,0:T(8,128)(2,1)}, u32[]{:S(2)}, u32[]{:S(2)}) async-start(bf16[64,8,3072]{2,1,0:T(8,128)(2,1)} %bitcast.228), calls=%async_computation | async-start | bytes 6291456 | tf_op jit(solution)/shard_map/all_to_all | solution.py:551
  181.0 6.6 %convolution_convert_fusion.3.act_grad_ref = bf16[768,1024]{1,0:T(8,128)(2,1)} fusion(bf16[768,2048]{1,0:T(8,128)(2,1)} %shard_map.340, bf16[1,1024,2048]{2,1,0:T(8,128)(2,1)S(1)} %copy-done.20), kind=kOutput, calls=%fused_computation.24 | convolution fusion | flops 3222011904 | bytes 8912896 | tf_op jit(solution)/shard_map/dot_general | solution.py:146
  189.5 8.0 %shard_map.336.both_w_ref = bf16[2048,2048]{1,0:T(8,128)(2,1)} custom-call(s32[3,64]{1,0:T(4,128)} %copy-done.12, bf16[512,768]{1,0:T(8,128)(2,1)} %copy-done.41, bf16[512,768]{1,0:T(8,128)(2,1)} %copy-done.39, bf16[512,768]{1,0:T(8,128)(2,1)} %copy-done.40, bf16[512,768]{1,0:T(8,128)(2,1)} %copy-done.42, bf16[512,640]{1,0:T(8,128)(2,1)} %copy-done.47, ...), custom_call_target="tpu_custom_call" | custom-call | tf_op jit(solution)/shard_map/pallas_call | solution.py:82
  197.5 15.2 %all-to-all-done = bf16[64,8,3072]{2,1,0:T(8,128)(2,1)} async-done(((bf16[64,8,3072]{2,1,0:T(8,128)(2,1)}), bf16[64,8,3072]{2,1,0:T(8,128)(2,1)}, u32[]{:S(2)}, u32[]{:S(2)}) %all-to-all-start) | async-done | bytes 3145760 | tf_op jit(solution)/shard_map/all_to_all | solution.py:551
  212.7 25.3 %shard_map.341 = (bf16[512,3072]{1,0:T(8,128)(2,1)}, bf16[768,2048]{1,0:T(8,128)(2,1)}, bf16[2,768,512]{2,1,0:T(8,128)(2,1)}, bf16[2,768,512]{2,1,0:T(8,128)(2,1...) custom-call(s32[1]{0:T(128)} %bitcast.25.core_ref, f32[1,64]{1,0:T(1,128)} %compare_convert_fusion.1.mine_ref, ...), custom_call_target="tpu_custom_call" | custom-call | flops 12884901888 | bytes 25165824 | tf_op jit(solution)/shard_map/pallas_call | solution.py:378
  238.0 10.6 %all-to-all-start.2 = ((bf16[64,8,3072]{2,1,0:T(8,128)(2,1)}), bf16[64,8,3072]{2,1,0:T(8,128)(2,1)}, u32[]{:S(2)}, u32[]{:S(2)}) async-start(bf16[64,8,3072]{2,1,0:T(8,128)(2,1)} %bitcast.235), calls=%async_computation.2 | async-start | bytes 6291456 | tf_op jit(solution)/shard_map/all_to_all | solution.py:551
  248.6 5.5 %convolution_convert_fusion = bf16[512,2048]{1,0:T(8,128)(2,1)} fusion(bf16[768,2048]{1,0:T(8,128)(2,1)} %shard_map.340, bf16[2,768,512]{2,1,0:T(8,128)(2,1)} %get-tuple-element.105.act_ref), kind=kOutput, calls=%fused_computation.6 | convolution fusion | flops 1611661312 | bytes 6029312 | tf_op jit(solution)/shard_map/dot_general | solution.py:140
  273.7 8.4 %shard_map.342 = bf16[512,3328]{1,0:T(8,128)(2,1)} custom-call(s32[1]{0:T(128)} %bitcast.25.core_ref, bf16[2,768,512]{2,1,0:T(8,128)(2,1)} %get-tuple-element.105.act_ref, bf16[1024,2048]{1,0:T(8,128)(2,1)} %bitcast.223, bf16[1024,2048]{1,0:T(8,128)(2,1)} %bitcast.224, bf16[512,256]{1,0:T(8,128)(2,1)} %pad.8.extra_ref), custom_call_target="tpu_custom_call" | custom-call | flops 3221225472 | bytes 12582912 | tf_op jit(solution)/shard_map/pallas_call | solution.py:297
  300.6 9.0 %all-to-all-start.3 = ((bf16[64,8,3328]{2,1,0:T(8,128)(2,1)}), bf16[64,8,3328]{2,1,0:T(8,128)(2,1)}, u32[]{:S(2)}, u32[]{:S(2)}) async-start(bf16[64,8,3328]{2,1,0:T(8,128)(2,1)} %bitcast.225), calls=%async_computation.3 | async-start | bytes 6815744 | tf_op jit(solution)/shard_map/all_to_all | solution.py:551
  343.9 11.0 %shard_map.346 = (f32[128,2048]{1,0:T(8,128)}, bf16[128,2048]{1,0:T(8,128)(2,1)}, f32[1,2048]{1,0:T(1,128)}) custom-call(s32[1]{0:T(128)} %bitcast.25.core_ref, bf16[256,1024]{1,0:T(8,128)(2,1)} %copy-done.4, bf16[256,1024]{1,0:T(8,128)(2,1)} %copy-done.3, bf16[256,1024]{1,0:T(8,128)(2,1)} %copy-done.2, bf16[256,2048]{1,0:T(8,128)(2,1)} %pad_maximum_fusion.6.scaled_ref, ...), custom_call_target="tpu_custom_call" | custom-call | flops 4000000000 | bytes 16777216 | tf_op jit(solution)/shard_map/pallas_call | solution.py:642
  359.3 6.4 %convert_add_fusion = f32[512,2048]{1,0:T(8,128)} fusion(bf16[512,2048]{1,0:T(8,128)(2,1)} %collective-permute-done.20, bf16[768,2048]{1,0:T(8,128)(2,1)} %shard_map.340, bf16[2,768,512]{2,1,0:T(8,128)(2,1)S(1)} %copy-done.31), kind=kOutput, calls=%fused_computation.3 | convolution fusion | flops 1612709888 | bytes 10223616 | tf_op jit(solution)/shard_map/dot_general | solution.py:140
  365.7 5.6 %convert_add_fusion.1 = f32[2048,512]{1,0:T(8,128)} fusion(bf16[2048,512]{1,0:T(8,128)(2,1)} %collective-permute-done.19, bf16[768,2048]{1,0:T(8,128)(2,1)S(1)} %copy-done.44, bf16[2,768,512]{2,1,0:T(8,128)(2,1)S(1)} %copy-done.111), kind=kOutput, calls=%fused_computation.4 | convolution fusion | flops 1612709888 | bytes 10223616 | tf_op jit(solution)/shard_map/dot_general | solution.py:140
  371.3 5.5 %convert_add_fusion.2 = f32[2048,512]{1,0:T(8,128)} fusion(bf16[2048,512]{1,0:T(8,128)(2,1)} %collective-permute-done.18, bf16[768,2048]{1,0:T(8,128)(2,1)S(1)} %copy-done.44, bf16[2,768,512]{2,1,0:T(8,128)(2,1)S(1)} %copy-done.109), kind=kOutput, calls=%fused_computation.5 | convolution fusion | flops 1612709888 | bytes 10223616 | tf_op jit(solution)/shard_map/dot_general | solution.py:140
  382.6 5.7 %shard_map.347 = (bf16[16,32,1408]{2,1,0:T(8,128)(2,1)}, bf16[16,32,1408]{2,1,0:T(8,128)(2,1)}, bf16[16,32,1280]{2,1,0:T(8,128)(2,1)}) custom-call(bf16[2048,256]{1,0:T(8,128)(2,1)} %bitcast.198, bf16[2048,256]{1,0:T(8,128)(2,1)} %bitcast.205, bf16[2048,256]{1,0:T(8,128)(2,1)} %bitcast.202, bf16[256,1024]{1,0:T(8,128)(2,1)} %copy-done.4, ...), custom_call_target="tpu_custom_call" | custom-call | tf_op jit(solution)/shard_map/pallas_call | solution.py:468
  396.9 10.3 %collective-permute-done.28.refs_15_.refs_12_ = bf16[16,32,1280]{2,1,0:T(8,128)(2,1)S(1)} collective-permute-done((bf16[16,32,1280]{2,1,0:T(8,128)(2,1)}, bf16[16,32,1280]{2,1,0:T(8,128)(2,1)S(1)}, u32[]{:S(2)}, u32[]{:S(2)}) %collective-permute-start.28) | collective-permute-done | bytes 1310752 | tf_op jit(solution)/shard_map/ppermute | solution.py:37
  408.6 6.0 %collective-permute-start.29 = (bf16[128,2048]{1,0:T(8,128)(2,1)}, bf16[128,2048]{1,0:T(8,128)(2,1)S(1)}, u32[]{:S(2)}, u32[]{:S(2)}) collective-permute-start(bf16[128,2048]{1,0:T(8,128)(2,1)} %get-tuple-element.145), channel_id=1, source_target_pairs={{0,64},{64,0},{1,65},{65,1},{2,66},{66,2},{3,67},{67,3},{4,68},{68... | collective-permute-start | bytes 1572872 | tf_op jit(solution)/shard_map/ppermute | solution.py:109
  422.4 9.9 %collective-permute-done.34.refs_13_ = bf16[8,32,1280]{2,1,0:T(8,128)(2,1)} collective-permute-done((bf16[8,32,1280]{2,1,0:T(8,128)(2,1)}, bf16[8,32,1280]{2,1,0:T(8,128)(2,1)}, u32[]{:S(2)}, u32[]{:S(2)}) %collective-permute-start.34) | collective-permute-done | bytes 655392 | tf_op jit(solution)/shard_map/ppermute | solution.py:37
  432.3 6.3 %shard_map.350 = bf16[8,32,4096]{2,1,0:T(8,128)(2,1)} custom-call(s32[1]{0:T(128)} %bitcast.69.place_ref, bf16[2048,256]{1,0:T(8,128)(2,1)} %bitcast.200, bf16[256,1024]{1,0:T(8,128)(2,1)} %copy-done.4, bf16[256,1024]{1,0:T(8,128)(2,1)} %copy-done.3, bf16[256,1024]{1,0:T(8,128)(2,1)} %copy-done.2, bf16[1024,256]{1,0:T(8,128)(2,1)} %bitcast.210, ...), custom_call_target="tpu_custom_call" | custom-call | tf_op jit(solution)/shard_map/pallas_call | solution.py:502
  457.5 8.0 %collective-permute-start.31 = (f32[72,1024]{0,1:T(8,128)S(1)}, f32[72,1024]{0,1:T(8,128)S(1)}, u32[]{:S(2)}, u32[]{:S(2)}) collective-permute-start(f32[72,1024]{0,1:T(8,128)S(1)} %pad_maximum_fusion.14), channel_id=1, source_target_pairs={{0,64},{64,0},{1,65},{65,1},{2,66},{66,2},{3,67},{67,3},{4,68},{68... | collective-permute-start | bytes 884744 | tf_op jit(solution)/shard_map/ppermute | solution.py:109
  (453 shorter events, 247.9 us)
Async XLA Ops:
  7.3 127.3 %all-gather.3.cloned.1.call-start = ((), (), s32[]{:S(2)}) async-start(), calls=%async_computation.5 | async-start | bytes 8519680 | tf_op jit(solution)/shard_map/all_gather | solution.py:703
  13.0 24.4 %collective-permute-start = (bf16[128,2048]{1,0:T(8,128)(2,1)S(1)}, bf16[128,2048]{1,0:T(8,128)(2,1)S(1)}, u32[]{:S(2)}, u32[]{:S(2)}) collective-permute-start(bf16[128,2048]{1,0:T(8,128)(2,1)S(1)} %get-tuple-element.277), channel_id=1, source_target_pairs={{0,64},{64,0},{1,65},{65,1},{2,66},{66,2},{3,67},{67,3},{4,68},{68... | collective-permute-start | bytes 1572872 | tf_op jit(solution)/shard_map/ppermute | solution.py:109
  47.4 25.4 %collective-permute-start.13 = (bf16[512,640]{1,0:T(8,128)(2,1)S(1)}, bf16[512,640]{1,0:T(8,128)(2,1)S(1)}, u32[]{:S(2)}, u32[]{:S(2)}) collective-permute-start(bf16[512,640]{1,0:T(8,128)(2,1)S(1)} %pad_maximum_fusion.10.refs_8_), channel_id=1, source_target_pairs={{0,3},{1,2},{2,1},{3,0},{4,7},{5,6},{6,5},{7,4},{8,11},{9,10},{10,... | collective-permute-start | bytes 1966088 | tf_op jit(solution)/shard_map/ppermute | solution.py:37
  51.9 24.4 %collective-permute-start.14 = (bf16[512,640]{1,0:T(8,128)(2,1)S(1)}, bf16[512,640]{1,0:T(8,128)(2,1)S(1)}, u32[]{:S(2)}, u32[]{:S(2)}) collective-permute-start(bf16[512,640]{1,0:T(8,128)(2,1)S(1)} %pad_maximum_fusion.10.refs_8_), channel_id=1, source_target_pairs={{0,12},{1,13},{2,14},{3,15},{4,8},{5,9},{6,10},{7,11},{8,4},{9,5},... | collective-permute-start | bytes 1966088 | tf_op jit(solution)/shard_map/ppermute | solution.py:37
  54.7 22.4 %collective-permute-start.5 = (bf16[512,768]{1,0:T(8,128)(2,1)S(1)}, bf16[512,768]{1,0:T(8,128)(2,1)S(1)}, u32[]{:S(2)}, u32[]{:S(2)}) collective-permute-start(bf16[512,768]{1,0:T(8,128)(2,1)S(1)} %pad_maximum_fusion.7.refs_0_), channel_id=1, source_target_pairs={{0,12},{1,13},{2,14},{3,15},{4,8},{5,9},{6,10},{7,11},{8,4},{9,5},... | collective-permute-start | bytes 2359304 | tf_op jit(solution)/shard_map/ppermute | solution.py:37
  60.0 19.1 %collective-permute-start.6 = (bf16[512,768]{1,0:T(8,128)(2,1)S(1)}, bf16[512,768]{1,0:T(8,128)(2,1)S(1)}, u32[]{:S(2)}, u32[]{:S(2)}) collective-permute-start(bf16[512,768]{1,0:T(8,128)(2,1)S(1)} %pad_maximum_fusion.7.refs_0_), channel_id=1, source_target_pairs={{0,48},{1,49},{2,50},{3,51},{4,52},{5,53},{6,54},{7,55},{8,56},{9,... | collective-permute-start | bytes 2359304 | tf_op jit(solution)/shard_map/ppermute | solution.py:37
  63.7 30.2 %collective-permute-start.11 = (bf16[512,640]{1,0:T(8,128)(2,1)S(1)}, bf16[512,640]{1,0:T(8,128)(2,1)S(1)}, u32[]{:S(2)}, u32[]{:S(2)}) collective-permute-start(bf16[512,640]{1,0:T(8,128)(2,1)S(1)} %collective-permute-done.9.refs_5_), channel_id=1, source_target_pairs={{0,3},{1,2},{2,1},{3,0},{4,7},{5,6},{6,5},{7,4},{8,11},{9,10},{10,... | collective-permute-start | bytes 1966088 | tf_op jit(solution)/shard_map/ppermute | solution.py:37
  72.9 24.1 %collective-permute-start.15 = (bf16[512,640]{1,0:T(8,128)(2,1)S(1)}, bf16[512,640]{1,0:T(8,128)(2,1)S(1)}, u32[]{:S(2)}, u32[]{:S(2)}) collective-permute-start(bf16[512,640]{1,0:T(8,128)(2,1)S(1)} %collective-permute-done.13.refs_9_), channel_id=1, source_target_pairs={{0,12},{1,13},{2,14},{3,15},{4,8},{5,9},{6,10},{7,11},{8,4},{9,5},... | collective-permute-start | bytes 1966088 | tf_op jit(solution)/shard_map/ppermute | solution.py:37
  77.2 25.1 %collective-permute-start.7 = (bf16[512,768]{1,0:T(8,128)(2,1)S(1)}, bf16[512,768]{1,0:T(8,128)(2,1)S(1)}, u32[]{:S(2)}, u32[]{:S(2)}) collective-permute-start(bf16[512,768]{1,0:T(8,128)(2,1)S(1)} %collective-permute-done.5.refs_1_), channel_id=1, source_target_pairs={{0,48},{1,49},{2,50},{3,51},{4,52},{5,53},{6,54},{7,55},{8,56},{9,... | collective-permute-start | bytes 2359304 | tf_op jit(solution)/shard_map/ppermute | solution.py:37
  117.6 48.1 %all-to-all-start.1 = ((bf16[64,8,3072]{2,1,0:T(8,128)(2,1)}), bf16[64,8,3072]{2,1,0:T(8,128)(2,1)}, u32[]{:S(2)}, u32[]{:S(2)}) async-start(bf16[64,8,3072]{2,1,0:T(8,128)(2,1)} %bitcast.227), calls=%async_computation.1 | async-start | bytes 6291456 | tf_op jit(solution)/shard_map/all_to_all | solution.py:551
  165.7 47.0 %all-to-all-start = ((bf16[64,8,3072]{2,1,0:T(8,128)(2,1)}), bf16[64,8,3072]{2,1,0:T(8,128)(2,1)}, u32[]{:S(2)}, u32[]{:S(2)}) async-start(bf16[64,8,3072]{2,1,0:T(8,128)(2,1)} %bitcast.228), calls=%async_computation | async-start | bytes 6291456 | tf_op jit(solution)/shard_map/all_to_all | solution.py:551
  238.0 49.4 %all-to-all-start.2 = ((bf16[64,8,3072]{2,1,0:T(8,128)(2,1)}), bf16[64,8,3072]{2,1,0:T(8,128)(2,1)}, u32[]{:S(2)}, u32[]{:S(2)}) async-start(bf16[64,8,3072]{2,1,0:T(8,128)(2,1)} %bitcast.235), calls=%async_computation.2 | async-start | bytes 6291456 | tf_op jit(solution)/shard_map/all_to_all | solution.py:551
  254.1 28.0 %collective-permute-start.20 = (bf16[512,2048]{1,0:T(8,128)(2,1)}, bf16[512,2048]{1,0:T(8,128)(2,1)}, u32[]{:S(2)}, u32[]{:S(2)}) collective-permute-start(bf16[512,2048]{1,0:T(8,128)(2,1)} %convolution_convert_fusion), channel_id=1, source_target_pairs={{0,64},{64,0},{1,65},{65,1},{2,66},{66,2},{3,67},{67,3},{4,68},{68... | collective-permute-start | bytes 6291464 | tf_op jit(solution)/shard_map/ppermute | solution.py:109
  258.6 23.5 %collective-permute-start.19 = (bf16[2048,512]{1,0:T(8,128)(2,1)}, bf16[2048,512]{1,0:T(8,128)(2,1)}, u32[]{:S(2)}, u32[]{:S(2)}) collective-permute-start(bf16[2048,512]{1,0:T(8,128)(2,1)} %convolution_convert_fusion.1), channel_id=1, source_target_pairs={{0,64},{64,0},{1,65},{65,1},{2,66},{66,2},{3,67},{67,3},{4,68},{68... | collective-permute-start | bytes 6291464 | tf_op jit(solution)/shard_map/ppermute | solution.py:109
  261.8 20.3 %collective-permute-start.18 = (bf16[2048,512]{1,0:T(8,128)(2,1)}, bf16[2048,512]{1,0:T(8,128)(2,1)}, u32[]{:S(2)}, u32[]{:S(2)}) collective-permute-start(bf16[2048,512]{1,0:T(8,128)(2,1)} %convolution_convert_fusion.2), channel_id=1, source_target_pairs={{0,64},{64,0},{1,65},{65,1},{2,66},{66,2},{3,67},{67,3},{4,68},{68... | collective-permute-start | bytes 6291464 | tf_op jit(solution)/shard_map/ppermute | solution.py:109
  265.9 32.4 %collective-permute-start.25 = (bf16[128,2048]{1,0:T(8,128)(2,1)}, bf16[128,2048]{1,0:T(8,128)(2,1)}, u32[]{:S(2)}, u32[]{:S(2)}) collective-permute-start(bf16[128,2048]{1,0:T(8,128)(2,1)} %get-tuple-element.276), channel_id=1, source_target_pairs={{0,64},{64,0},{1,65},{65,1},{2,66},{66,2},{3,67},{67,3},{4,68},{68... | collective-permute-start | bytes 1572872 | tf_op jit(solution)/shard_map/ppermute | solution.py:109
  300.6 76.2 %all-to-all-start.3 = ((bf16[64,8,3328]{2,1,0:T(8,128)(2,1)}), bf16[64,8,3328]{2,1,0:T(8,128)(2,1)}, u32[]{:S(2)}, u32[]{:S(2)}) async-start(bf16[64,8,3328]{2,1,0:T(8,128)(2,1)} %bitcast.225), calls=%async_computation.3 | async-start | bytes 6815744 | tf_op jit(solution)/shard_map/all_to_all | solution.py:551
  309.6 137.8 %all-gather.5.cloned.1.call-start = ((), (), s32[]{:S(2)}) async-start(), calls=%async_computation.6 | async-start | bytes 1597440 | tf_op jit(solution)/shard_map/all_gather | solution.py:939
  339.4 41.2 %collective-permute-start.22 = (bf16[32,32,1408]{2,1,0:T(8,128)(2,1)}, bf16[32,32,1408]{2,1,0:T(8,128)(2,1)}, u32[]{:S(2)}, u32[]{:S(2)}) collective-permute-start(bf16[32,32,1408]{2,1,0:T(8,128)(2,1)} %get-tuple-element.121), channel_id=1, source_target_pairs={{0,48},{1,49},{2,50},{3,51},{4,52},{5,53},{6,54},{7,55},{8,56},{9,... | collective-permute-start | bytes 8650760 | tf_op jit(solution)/shard_map/ppermute | solution.py:37
  340.6 40.0 %collective-permute-start.23 = (bf16[32,32,1408]{2,1,0:T(8,128)(2,1)S(1)}, bf16[32,32,1408]{2,1,0:T(8,128)(2,1)}, u32[]{:S(2)}, u32[]{:S(2)}) collective-permute-start(bf16[32,32,1408]{2,1,0:T(8,128)(2,1)S(1)} %get-tuple-element.122), channel_id=1, source_target_pairs={{0,3},{1,2},{2,1},{3,0},{4,7},{5,6},{6,5},{7,4},{8,11},{9,10},{10,... | collective-permute-start | bytes 8650760 | tf_op jit(solution)/shard_map/ppermute | solution.py:37
  342.6 34.2 %collective-permute-start.24 = (bf16[32,32,1280]{2,1,0:T(8,128)(2,1)S(1)}, bf16[32,32,1280]{2,1,0:T(8,128)(2,1)}, u32[]{:S(2)}, u32[]{:S(2)}) collective-permute-start(bf16[32,32,1280]{2,1,0:T(8,128)(2,1)S(1)} %get-tuple-element.123), channel_id=1, source_target_pairs={{0,12},{1,13},{2,14},{3,15},{4,8},{5,9},{6,10},{7,11},{8,4},{9,5},... | collective-permute-start | bytes 7864328 | tf_op jit(solution)/shard_map/ppermute | solution.py:37
  355.7 21.1 %collective-permute-start.30 = (f32[4,1024]{1,0:T(4,128)S(1)}, f32[4,1024]{1,0:T(4,128)S(1)}, u32[]{:S(2)}, u32[]{:S(2)}) collective-permute-start(f32[4,1024]{1,0:T(4,128)S(1)} %constant_dynamic-slice_fusion), channel_id=1, source_target_pairs={{0,64},{64,0},{1,65},{65,1},{2,66},{66,2},{3,67},{67,3},{4,68},{68... | collective-permute-start | bytes 49160 | tf_op jit(solution)/shard_map/ppermute | solution.py:109
  388.3 18.9 %collective-permute-start.26 = (bf16[16,32,1408]{2,1,0:T(8,128)(2,1)}, bf16[16,32,1408]{2,1,0:T(8,128)(2,1)S(1)}, u32[]{:S(2)}, u32[]{:S(2)}) collective-permute-start(bf16[16,32,1408]{2,1,0:T(8,128)(2,1)} %get-tuple-element.137), channel_id=1, source_target_pairs={{0,12},{1,13},{2,14},{3,15},{4,8},{5,9},{6,10},{7,11},{8,4},{9,5},... | collective-permute-start | bytes 4325384 | tf_op jit(solution)/shard_map/ppermute | solution.py:37
  438.6 35.5 %all-to-all-start.4 = ((bf16[8,32,4096]{2,1,0:T(8,128)(2,1)}), bf16[8,32,4096]{2,1,0:T(8,128)(2,1)}, u32[]{:S(2)}, u32[]{:S(2)}) async-start(bf16[8,32,4096]{2,1,0:T(8,128)(2,1)} %shard_map.350), calls=%async_computation.4 | async-start | bytes 4194304 | tf_op jit(solution)/shard_map/all_to_all | solution.py:913
  (132 other events, 1061.8 us)
Sparse Core Ops, SparseCore 0:
  11.6 92.0 all-gather.2
  382.8 64.6 all-gather.4
